TPU v7x, 128 devices: a whole 4x4x4 slice. The times are simulated.
128 devices in a mesh: row: 8 (over x, core), col: 16 (over y, z).
Axes of the slice: x: 4, y: 4, z: 4, core: 2. Of those that a mesh axis runs over, the one named last changes fastest.
Arguments:
- nodes: bfloat16 [8192, 512], P(('row', 'col')), may hold values from -6 to 6
- edges: bfloat16 [8, 16, 4096, 512], P('row', 'col'), may hold values from -6 to 6
- senders: int32 [8, 16, 4096], P('row', 'col'), may hold values from 0 to 511
- receivers: int32 [8, 16, 4096], P('row', 'col'), may hold values from 0 to 1023
- levels: int32 [8, 16, 4096], P('row', 'col'), may hold values from 0 to 6
- counts: int32 [8, 16], P('row', 'col'), may hold values from 1 to 4096, as said below
- edge_w1: bfloat16 [3, 512, 512], replicated, may hold values from -0.15625 to 0.15625
- level_bias: bfloat16 [7, 512], replicated, may hold values from -6 to 6
- edge_w2: bfloat16 [512, 512], replicated, may hold values from -0.25 to 0.25
- edge_gain: float32 [512], replicated, may hold values from 0.1 to 1.9
- node_w1: bfloat16 [2, 512, 512], replicated, may hold values from -0.1875 to 0.1875
- node_w2: bfloat16 [512, 512], replicated, may hold values from -0.25 to 0.25
- node_gain: float32 [512], replicated, may hold values from 0.1 to 1.9
- grid: bfloat16 [131072, 512], P(('row', 'col')), may hold values from -6 to 6
- send_rows: int32 [128, 128, 4], P(('row', 'col')), may hold values from 0 to 63, as said below
- dec_index: int32 [131072, 3], P(('row', 'col')), may hold values from 0 to 511, as said below
- dec_w1: bfloat16 [2, 512, 512], replicated, may hold values from -0.1875 to 0.1875
- dec_w2: bfloat16 [512, 512], replicated, may hold values from -0.25 to 0.25
- dec_gain: float32 [512], replicated, may hold values from 0.1 to 1.9
Outputs:
- nodes_out: bfloat16 [8192, 512], P(('row', 'col'))
- edges_out: bfloat16 [8, 16, 4096, 512], P('row', 'col')
- grid_out: bfloat16 [131072, 512], P(('row', 'col'))
Inputs may be any that keep to these rules, and one draw needn't show every extreme that they name: `senders`: at slots at or beyond the tile's count the index is arbitrary and unused. `receivers`: at slots at or beyond the tile's count the index is arbitrary and unused. `counts`: some tile is full in every draw. `send_rows`: the 4 rows that one device sends to one band device are distinct. `dec_index`: buffer rows are laid out by source device, then slot; every row of a band's buffer is named by some decoder edge of that band.
All inputs are finite; a program needn't handle non-finite values.
Results may differ from a plain program's by a relative error of at most 0.015.
Values may be sent and summed in bfloat16 or wider, within the bound.
No kernel may reach another device: no remote copies, remote signals or barrier semaphores. Data moves between devices by JAX's collectives and lax.ppermute only.
A program may use at most 128 MiB of HBM per device.

v0:
```python
import math

import jax
import jax.numpy as jnp
from jax import lax
from jax.sharding import PartitionSpec as P

EPSILON = 1e-05


def layer_norm(values, gain):
    center = values - jnp.mean(values, axis=-1, keepdims=True)
    spread = jnp.mean(center * center, axis=-1, keepdims=True)
    return center * lax.rsqrt(spread + EPSILON) * gain


def mlp_tail(pre, second_weight, gain):
    hidden = jax.nn.silu(pre).astype(jnp.bfloat16)
    output = jnp.dot(hidden, second_weight, preferred_element_type=jnp.float32)
    return layer_norm(output, gain)


def one_hot_rows(ids, count):
    return (ids[:, None] == jnp.arange(count, dtype=jnp.int32)[None, :]).astype(jnp.bfloat16)


def select_low(table_hot, table):
    return jnp.dot(table_hot, table, preferred_element_type=jnp.float32).astype(jnp.bfloat16)


def on_device(
    nodes,
    edges,
    senders,
    receivers,
    levels,
    counts,
    edge_w1,
    level_bias,
    edge_w2,
    edge_gain,
    node_w1,
    node_w2,
    node_gain,
    grid,
    send_rows,
    dec_index,
    dec_w1,
    dec_w2,
    dec_gain,
):
    node_block = nodes.shape[0]
    width = nodes.shape[1]
    capacity = edges.shape[2]
    level_count = level_bias.shape[0]
    sender_count = node_block * lax.axis_size("row")
    receiver_count = node_block * lax.axis_size("col")
    sender_block = lax.all_gather(nodes, "row", axis=0, tiled=True)
    receiver_block = lax.all_gather(nodes, "col", axis=0, tiled=True)
    joined_weight = edge_w1.reshape(3 * width, width)

    def first_layer(rows, send_hot, recv_hot):
        joined = jnp.concatenate(
            [rows, select_low(send_hot, sender_block), select_low(recv_hot, receiver_block)], axis=1
        )
        return jnp.dot(joined, joined_weight, preferred_element_type=jnp.float32)

    block_rows = math.gcd(capacity, 1024)
    block_count = capacity // block_rows
    slot_used = jnp.arange(capacity, dtype=jnp.int32) < counts[0, 0]
    items = (
        edges[0, 0].reshape(block_count, block_rows, width),
        senders[0, 0].reshape(block_count, block_rows),
        receivers[0, 0].reshape(block_count, block_rows),
        levels[0, 0].reshape(block_count, block_rows),
        slot_used.reshape(block_count, block_rows),
    )

    def edge_block(partial_value, item):
        rows, send_ids, recv_ids, level_ids, used = item
        send_hot = one_hot_rows(send_ids, sender_count)
        recv_hot = one_hot_rows(recv_ids, receiver_count)
        pre = first_layer(rows, send_hot, recv_hot)
        pre = pre + jnp.dot(
            one_hot_rows(level_ids, level_count), level_bias, preferred_element_type=jnp.float32
        )
        message = mlp_tail(pre, edge_w2, edge_gain).astype(jnp.bfloat16)
        kept = jnp.where(used[:, None], message, jnp.zeros((), jnp.bfloat16))
        updated = (rows.astype(jnp.float32) + kept.astype(jnp.float32)).astype(jnp.bfloat16)
        partial_value = partial_value + lax.dot_general(
            recv_hot, kept, (((0,), (0,)), ((), ())), preferred_element_type=jnp.float32
        )
        return (partial_value, updated)

    partial_value, edge_new = lax.scan(
        edge_block, jnp.zeros((receiver_count, width), jnp.float32), items
    )
    edges_out = edge_new.reshape(1, 1, capacity, width)
    summed = lax.psum(partial_value.astype(jnp.bfloat16), "col").astype(jnp.float32)
    aggregated = lax.dynamic_slice_in_dim(summed, lax.axis_index("col") * node_block, node_block, 0)
    node_pre = jnp.dot(nodes, node_w1[0], preferred_element_type=jnp.float32)
    node_pre = node_pre + jnp.dot(
        aggregated.astype(jnp.bfloat16), node_w1[1], preferred_element_type=jnp.float32
    )
    nodes_out = (nodes.astype(jnp.float32) + mlp_tail(node_pre, node_w2, node_gain)).astype(
        jnp.bfloat16
    )
    peers = send_rows.shape[1]
    per_peer = send_rows.shape[2]
    picked = select_low(one_hot_rows(send_rows[0].reshape(-1), node_block), nodes_out).reshape(
        peers, per_peer, width
    )
    received = lax.all_to_all(picked, ("row", "col"), split_axis=0, concat_axis=0, tiled=True)
    cells = grid.shape[0]
    fan_count = dec_index.shape[1]
    chosen = select_low(
        one_hot_rows(dec_index.reshape(-1), peers * per_peer),
        received.reshape(peers * per_peer, width),
    )
    node_dec = jnp.dot(chosen, dec_w1[1], preferred_element_type=jnp.float32).reshape(
        cells, fan_count, width
    )
    grid_part = jnp.dot(grid, dec_w1[0], preferred_element_type=jnp.float32)
    dec_pre = grid_part[:, None, :] + node_dec
    messages = mlp_tail(dec_pre.reshape(cells * fan_count, width), dec_w2, dec_gain).reshape(
        cells, fan_count, width
    )
    grid_out = (grid.astype(jnp.float32) + jnp.sum(messages, axis=1)).astype(jnp.bfloat16)
    return (nodes_out, edges_out, grid_out)


def solution(mesh):
    return jax.shard_map(
        on_device,
        mesh=mesh,
        in_specs=(
            P(("row", "col"), None),
            P("row", "col", None, None),
            P("row", "col", None),
            P("row", "col", None),
            P("row", "col", None),
            P("row", "col"),
            P(),
            P(),
            P(),
            P(),
            P(),
            P(),
            P(),
            P(("row", "col"), None),
            P(("row", "col"), None, None),
            P(("row", "col"), None),
            P(),
            P(),
            P(),
        ),
        out_specs=(P(("row", "col"), None), P("row", "col", None, None), P(("row", "col"), None)),
        check_vma=False,
    )
```

profile of v0, /device:TPU:1, one launch (start us, length us, event | category | flops | bytes accessed | tf_op | source)
XLA Modules:
  0.0 344.8 jit_solution(2025392052135723121)
XLA Ops:
  13.4 15.0 %all_gather.6 = bf16[512,512]{1,0:T(8,128)(2,1)S(1)} all-gather(bf16[64,512]{1,0:T(8,128)(2,1)} %param.21), channel_id=1, replica_groups=mesh['row'=8,'col'=16] {'row'}, dimensions={0}, use_global_device_ids=true | all-gather | bytes 589824 | tf_op jit(solution)/shard_map/all_gather | solution.py:58
  28.4 26.4 %all-gather.2.cloned.1.call-done = bf16[1024,512]{1,0:T(8,128)(2,1)} async-done(((bf16[64,512]{1,0:T(8,128)(2,1)}), bf16[1024,512]{1,0:T(8,128)(2,1)}) %all-gather.2.cloned.1.call-update) | async-done | bytes 1048592 | tf_op jit(solution)/shard_map/all_gather | solution.py:59
  54.8 99.2 %while.13 = (s32[]{:T(128)}, f32[1024,512]{1,0:T(8,128)}, bf16[4,1024,512]{2,1,0:T(8,128)(2,1)}, s32[4,1024]{1,0:T(4,128)S(1)}, pred[4,1024]{1,0:T(4,128)(4,1)S(...) while((s32[]{:T(128)}, f32[1024,512]{1,0:T(8,128)}, ...), condition=%wide.region_3.4_spmd.clone, body=%wide.region_0.3_spmd.clone.sunk | while | flops 4866973696 | bytes 48897348 | solution.py:95
  62.1 5.2 %fusion.97 = f32[1024,512]{1,0:T(8,128)} fusion(bf16[1536,512]{1,0:T(8,128)(2,1)} %get-tuple-element.307, bf16[1024,512]{0,1:T(8,128)(2,1)} %fusion.95, bf16[1024,512]{0,1:T(8,128)(2,1)} %fusion.96, bf16[1024,512]{0,1:T(8,128)(2,1)S(1)} %bitcast.64), kind=kOutput, calls=%fused_computation.3.clone.1 | convolution fusion | flops 1620049920 | bytes 6815744 | tf_op jit(solution)/shard_map/while/body/eval_jaxpr/dot_general | solution.py:66
  72.9 3.0 select_add_fusion.2
  85.7 5.2 %fusion.97 = f32[1024,512]{1,0:T(8,128)} fusion(bf16[1536,512]{1,0:T(8,128)(2,1)} %get-tuple-element.307, bf16[1024,512]{0,1:T(8,128)(2,1)} %fusion.95, bf16[1024,512]{0,1:T(8,128)(2,1)} %fusion.96, bf16[1024,512]{0,1:T(8,128)(2,1)S(1)} %bitcast.64), kind=kOutput, calls=%fused_computation.3.clone.1 | convolution fusion | flops 1620049920 | bytes 6815744 | tf_op jit(solution)/shard_map/while/body/eval_jaxpr/dot_general | solution.py:66
  90.9 2.9 fusion.98
  96.5 4.6 %select_add_fusion.2 = f32[1024,512]{1,0:T(8,128)} fusion(f32[1024,512]{1,0:T(8,128)} %get-tuple-element.283, s32[1024]{0:T(1024)S(1)} %bitcast.67, pred[]{:T(512)S(6)} %compare.3, f32[1024,512]{0,1:T(8,128)S(1)} %get-tuple-element.264, f32[512]{0:T(512)S(1)} %copy-done.6, f32[1024]{0:T(1024)S(1)} %add_rsqrt_fusion.4, ...), kind=kOutput, calls=%fused_computation.10.clone.1 | convolution fusion | flops 1079508992 | bytes 6306817 | tf_op jit(solution)/shard_map/while/body/eval_jaxpr/dot_general | solution.py:90
  110.9 5.2 %fusion.97 = f32[1024,512]{1,0:T(8,128)} fusion(bf16[1536,512]{1,0:T(8,128)(2,1)} %get-tuple-element.307, bf16[1024,512]{0,1:T(8,128)(2,1)} %fusion.95, bf16[1024,512]{0,1:T(8,128)(2,1)} %fusion.96, bf16[1024,512]{0,1:T(8,128)(2,1)S(1)} %bitcast.64), kind=kOutput, calls=%fused_computation.3.clone.1 | convolution fusion | flops 1620049920 | bytes 6815744 | tf_op jit(solution)/shard_map/while/body/eval_jaxpr/dot_general | solution.py:66
  121.7 4.5 %select_add_fusion.2 = f32[1024,512]{1,0:T(8,128)} fusion(f32[1024,512]{1,0:T(8,128)} %get-tuple-element.283, s32[1024]{0:T(1024)S(1)} %bitcast.67, pred[]{:T(512)S(6)} %compare.3, f32[1024,512]{0,1:T(8,128)S(1)} %get-tuple-element.264, f32[512]{0:T(512)S(1)} %copy-done.6, f32[1024]{0:T(1024)S(1)} %add_rsqrt_fusion.4, ...), kind=kOutput, calls=%fused_computation.10.clone.1 | convolution fusion | flops 1079508992 | bytes 6306817 | tf_op jit(solution)/shard_map/while/body/eval_jaxpr/dot_general | solution.py:90
  136.1 5.2 %fusion.97 = f32[1024,512]{1,0:T(8,128)} fusion(bf16[1536,512]{1,0:T(8,128)(2,1)} %get-tuple-element.307, bf16[1024,512]{0,1:T(8,128)(2,1)} %fusion.95, bf16[1024,512]{0,1:T(8,128)(2,1)} %fusion.96, bf16[1024,512]{0,1:T(8,128)(2,1)S(1)} %bitcast.64), kind=kOutput, calls=%fused_computation.3.clone.1 | convolution fusion | flops 1620049920 | bytes 6815744 | tf_op jit(solution)/shard_map/while/body/eval_jaxpr/dot_general | solution.py:66
  146.9 4.6 %select_add_fusion.2 = f32[1024,512]{1,0:T(8,128)} fusion(f32[1024,512]{1,0:T(8,128)} %get-tuple-element.283, s32[1024]{0:T(1024)S(1)} %bitcast.67, pred[]{:T(512)S(6)} %compare.3, f32[1024,512]{0,1:T(8,128)S(1)} %get-tuple-element.264, f32[512]{0:T(512)S(1)} %copy-done.6, f32[1024]{0:T(1024)S(1)} %add_rsqrt_fusion.4, ...), kind=kOutput, calls=%fused_computation.10.clone.1 | convolution fusion | flops 1079508992 | bytes 6306817 | tf_op jit(solution)/shard_map/while/body/eval_jaxpr/dot_general | solution.py:90
  157.4 86.1 %all-reduce.2.cloned.1.call-done = bf16[1024,512]{1,0:T(8,128)(2,1)} async-done(((bf16[1024,512]{1,0:T(8,128)(2,1)}), bf16[1024,512]{1,0:T(8,128)(2,1)}) %all-reduce.2.cloned.1.call-update) | async-done | bytes 1048592 | tf_op jit(solution)/shard_map/psum | solution.py:99
  246.4 8.8 %all-to-all-start = ((bf16[128,4,512]{2,1,0:T(4,128)(2,1)}), bf16[128,4,512]{2,1,0:T(4,128)(2,1)S(1)}, u32[]{:S(2)}, u32[]{:S(2)}) async-start(bf16[128,4,512]{2,1,0:T(4,128)(2,1)} %reshape.80), calls=%async_computation | async-start | bytes 1048576 | tf_op jit(solution)/shard_map/all_to_all | solution.py:113
  257.8 11.3 %all-to-all-done = bf16[128,4,512]{2,1,0:T(4,128)(2,1)S(1)} async-done(((bf16[128,4,512]{2,1,0:T(4,128)(2,1)}), bf16[128,4,512]{2,1,0:T(4,128)(2,1)S(1)}, u32[]{:S(2)}, u32[]{:S(2)}) %all-to-all-start) | async-done | bytes 524320 | tf_op jit(solution)/shard_map/all_to_all | solution.py:113
  270.0 4.7 %fusion.28 = bf16[3072,512]{1,0:T(8,128)(2,1)} fusion(bf16[512,512]{1,0:T(8,128)(2,1)} %reshape.81, s32[3072]{0:T(1024)S(1)} %eq.75), kind=kOutput, calls=%fused_computation.43 | convolution fusion | flops 1613758464 | bytes 3682304 | tf_op jit(solution)/shard_map/dot_general | solution.py:28
  274.7 9.1 %dot_general.50 = bf16[1024,3,512]{2,1,0:T(4,128)(2,1)} reshape(bf16[3072,512]{1,0:T(8,128)(2,1)} %fusion.28) | data formatting | bytes 6291456 | tf_op jit(solution)/shard_map/dot_general | solution.py:120
  283.8 4.4 %broadcast_add_fusion = f32[1024,3,512]{2,0,1:T(8,128)S(1)} fusion(f32[1024,512]{1,0:T(8,128)S(1)} %fusion.36, bf16[1024,3,512]{2,1,0:T(4,128)(2,1)} %dot_general.50, bf16[2,512,512]{2,1,0:T(8,128)(2,1)} %param.37), kind=kOutput, calls=%fused_computation.47 | convolution fusion | flops 1612185600 | bytes 13107200 | tf_op jit(solution)/shard_map/dot_general | solution.py:120
  288.2 7.5 %copy.29 = f32[1024,3,512]{2,1,0:T(4,128)} copy(f32[1024,3,512]{2,0,1:T(8,128)S(1)} %broadcast_add_fusion) | data formatting | bytes 12582912 | tf_op jit(solution)/shard_map/add | solution.py:124
  295.8 10.8 %reshape.82 = f32[3072,512]{1,0:T(8,128)} reshape(f32[1024,3,512]{2,1,0:T(4,128)} %copy.29) | data formatting | bytes 12582912 | tf_op jit(solution)/shard_map/reshape | solution.py:125
  306.5 4.1 %fusion.62 = (f32[3072]{0:T(1024)S(1)}, f32[3072,512]{1,0:T(8,128)S(1)}) fusion(bf16[512,512]{1,0:T(8,128)(2,1)S(1)} %copy-done, f32[3072,512]{1,0:T(8,128)} %reshape.82), kind=kOutput, calls=%fused_computation.81 | convolution fusion | flops 1620046848 | bytes 13119488 | tf_op jit(solution)/shard_map/dot_general | solution.py:19
  312.7 3.8 %multiply_multiply_fusion = f32[3072,512]{1,0:T(8,128)} fusion(f32[3072,512]{1,0:T(8,128)S(1)} %get-tuple-element.172, f32[512]{0:T(512)S(1)} %copy-done.9, f32[3072]{0:T(1024)S(1)} %add_rsqrt_fusion.1, f32[3072]{0:T(1024)S(1)} %broadcast_multiply_fusion.1), kind=kLoop, calls=%fused_computation.38 | loop fusion | flops 4718592 | bytes 12609536 | tf_op jit(solution)/shard_map/mul | solution.py:14
  316.5 10.5 %reshape.83 = f32[1024,3,512]{2,1,0:T(4,128)} reshape(f32[3072,512]{1,0:T(8,128)} %multiply_multiply_fusion) | data formatting | bytes 12582912 | tf_op jit(solution)/shard_map/reshape | solution.py:125
  327.0 8.4 %reduce_sum.67 = f32[1024,512]{1,0:T(8,128)S(1)} reduce(f32[1024,3,512]{2,1,0:T(4,128)} %reshape.83, f32[]{:T(128)} %constant.51.clone.1), dimensions={1}, to_apply=%region_9.10 | reduce | flops 1048576 | bytes 8388612 | tf_op jit(solution)/shard_map/reduce_sum | solution.py:128
  (146 shorter events, 78.4 us)
Async XLA Ops:
  7.2 299.4 %copy-start = (bf16[512,512]{1,0:T(8,128)(2,1)S(1)}, bf16[512,512]{1,0:T(8,128)(2,1)}, u32[]{:S(2)}) copy-start(bf16[512,512]{1,0:T(8,128)(2,1)} %param.38) | copy-start | bytes 1572868
  7.2 47.6 %all-gather.2.cloned.1.call-start = ((), (), s32[]{:S(2)}) async-start(), calls=%async_computation.1 | async-start | bytes 1114112 | tf_op jit(solution)/shard_map/all_gather | solution.py:59
  7.9 235.5 %all-reduce.2.cloned.1.call-start = ((), (), s32[]{:S(2)}) async-start(), calls=%async_computation.2 | async-start | bytes 2097152 | tf_op jit(solution)/shard_map/psum | solution.py:99
  54.8 2.0 copy-start.11
  62.1 5.2 %copy-start.13 = (bf16[7,512]{1,0:T(8,128)(2,1)S(1)}, bf16[7,512]{1,0:T(8,128)(2,1)}, u32[]{:S(2)}) copy-start(bf16[7,512]{1,0:T(8,128)(2,1)} %get-tuple-element.309) | copy-start | bytes 21508 | tf_op jit(solution)/shard_map/while
  70.2 1.2 copy-start.2
  78.4 2.0 copy-start.11
  85.7 5.2 %copy-start.13 = (bf16[7,512]{1,0:T(8,128)(2,1)S(1)}, bf16[7,512]{1,0:T(8,128)(2,1)}, u32[]{:S(2)}) copy-start(bf16[7,512]{1,0:T(8,128)(2,1)} %get-tuple-element.309) | copy-start | bytes 21508 | tf_op jit(solution)/shard_map/while
  93.8 1.2 copy-start.2
  103.6 2.0 copy-start.11
  110.9 5.2 %copy-start.13 = (bf16[7,512]{1,0:T(8,128)(2,1)S(1)}, bf16[7,512]{1,0:T(8,128)(2,1)}, u32[]{:S(2)}) copy-start(bf16[7,512]{1,0:T(8,128)(2,1)} %get-tuple-element.309) | copy-start | bytes 21508 | tf_op jit(solution)/shard_map/while
  119.0 1.2 copy-start.2
  128.8 2.0 copy-start.11
  136.1 5.2 %copy-start.13 = (bf16[7,512]{1,0:T(8,128)(2,1)S(1)}, bf16[7,512]{1,0:T(8,128)(2,1)}, u32[]{:S(2)}) copy-start(bf16[7,512]{1,0:T(8,128)(2,1)} %get-tuple-element.309) | copy-start | bytes 21508 | tf_op jit(solution)/shard_map/while
  144.2 1.2 copy-start.2
  154.0 2.9 copy-start.10
  154.0 3.1 copy-start.3
  154.0 3.1 copy-start.4
  154.0 89.4 %copy-start.12 = (bf16[512,512]{1,0:T(8,128)(2,1)S(1)}, bf16[512,512]{1,0:T(8,128)(2,1)}, u32[]{:S(2)}) copy-start(bf16[512,512]{1,0:T(8,128)(2,1)} %param.32) | copy-start | bytes 1572868
  156.9 88.1 %copy-start.8 = (f32[512]{0:T(512)S(1)}, f32[512]{0:T(512)}, u32[]{:S(2)}) copy-start(f32[512]{0:T(512)} %param.33) | copy-start | bytes 6148
  157.4 97.9 %copy-start.7 = (s32[1024,3]{0,1:T(4,128)S(1)}, s32[1024,3]{0,1:T(4,128)}, u32[]{:S(2)}) copy-start(s32[1024,3]{0,1:T(4,128)} %param.36) | copy-start | bytes 36868
  245.1 12.7 %copy-start.5 = (bf16[64,512]{1,0:T(8,128)(2,1)}, bf16[64,512]{1,0:T(8,128)(2,1)S(1)}, u32[]{:S(2)}) copy-start(bf16[64,512]{1,0:T(8,128)(2,1)S(1)} %add_convert_fusion.2) | copy-start | bytes 196612
  246.4 22.7 %all-to-all-start = ((bf16[128,4,512]{2,1,0:T(4,128)(2,1)}), bf16[128,4,512]{2,1,0:T(4,128)(2,1)S(1)}, u32[]{:S(2)}, u32[]{:S(2)}) async-start(bf16[128,4,512]{2,1,0:T(4,128)(2,1)} %reshape.80), calls=%async_computation | async-start | bytes 1048576 | tf_op jit(solution)/shard_map/all_to_all | solution.py:113
  310.7 2.0 copy-start.9
  (8 other events, 8.9 us)
Sparse Core Ops, SparseCore 0:
  10.2 44.6 all-gather.1
  157.0 86.3 all-reduce.1
where the time goes:
time: 347 us; the launch traced here: 345 us
  waiting for transfers between devices  124 us (36%)
  matrix products  83.5 us (24%)
  local copies, waits for them, and re-layouts  66.4 us (19%)
  other arithmetic  31.3 us (9%)
  blocking collectives  15 us (4%)
  between operations  14.9 us (4%)
  starting transfers between devices  8.92 us (3%)
    psum x1, waiting for transfers between devices, on_device(): lax.psum(partial_value.astype(jnp.bfloat16), 'col').astype(jnp.float32)  86.1 us
    all_gather x1, waiting for transfers between devices, on_device(): receiver_block = lax.all_gather(nodes, 'col', axis=0, tiled=True)  26.4 us
    dot_general x10, matrix products, select_low(): jnp.dot(table_hot, table, preferred_element_type=jnp.float32)  22.4 us
    dot_general x4, matrix products, first_layer(): return jnp.dot(joined, joined_weight, preferred_element_type=jnp.float32)  20.7 us
    dot_general x6, matrix products, mlp_tail(): output = jnp.dot(hidden, second_weight, preferred_element_type=jnp.float32)  17.1 us
    dot_general x4, matrix products, edge_block(): lax.dot_general(recv_hot, kept, (((0,), (0,)), ((), ())), preferred_eleme...  16.6 us
    all_gather x1, blocking collectives, on_device(): sender_block = lax.all_gather(nodes, 'row', axis=0, tiled=True)  15 us
    all_to_all x1, waiting for transfers between devices, on_device(): lax.all_to_all(picked, ('row', 'col'), split_axis=0, concat_axis=0, tiled...  11.3 us
  transfers between devices with their start and end apart: 3, of which 3 were waited for; matrix products, arithmetic and copies ran while one was open for 2% of the time, Pallas kernels for 0%

commit v1 on v0

v1 whole, which is shorter than its diff:
```python
import functools

import jax
import jax.numpy as jnp
from jax import lax
from jax.experimental import pallas as pl
from jax.experimental.pallas import tpu as pltpu
from jax.sharding import PartitionSpec as P

EPSILON = 1e-05
LANES = 128
EDGE_ROWS = 512
CELL_ROWS = 256
VMEM_BYTES = 56 * 1024 * 1024


def dot(a, b):
    return jnp.dot(a, b, preferred_element_type=jnp.float32)


def silu_low(pre):
    half = 0.5 * pre
    return (half + half * jnp.tanh(half)).astype(jnp.bfloat16)


def center_scale(values):
    center = values - jnp.mean(values, axis=-1, keepdims=True)
    spread = jnp.mean(center * center, axis=-1, keepdims=True)
    return center, lax.rsqrt(spread + EPSILON)


def column_hot(ids, count):
    lanes = lax.broadcasted_iota(jnp.int32, (ids.shape[0], count), 1)
    return (ids == lanes).astype(jnp.bfloat16)


def row_hot(ids, count):
    rows = lax.broadcasted_iota(jnp.int32, (count, ids.shape[1]), 0)
    return (ids == rows).astype(jnp.bfloat16)


def project_kernel(nodes_ref, weight_ref, send_ref, recv_ref):
    nodes = nodes_ref[...]
    send = dot(nodes, weight_ref[1]).astype(jnp.bfloat16)
    recv = dot(nodes, weight_ref[2]).astype(jnp.bfloat16)
    for k in range(send_ref.shape[0]):
        send_ref[k] = send
    for k in range(recv_ref.shape[0]):
        recv_ref[k] = recv


def edge_kernel(
    count_ref,
    ids_ref,
    rows_ref,
    send_ref,
    recv_ref,
    w1_ref,
    bias_ref,
    w2_ref,
    gain_ref,
    out_ref,
    sum_ref,
    total,
):
    step = pl.program_id(0)
    rows = rows_ref.shape[0]
    parts = rows // LANES
    count = count_ref[0, 0]

    @pl.when(step == 0)
    def _():
        total[...] = jnp.zeros_like(total)

    @pl.when(step * rows >= count)
    def _():
        out_ref[...] = rows_ref[...]

    @pl.when(step * rows < count)
    def _():
        ids = ids_ref[0]
        columns = jnp.transpose(ids)

        def gather_hot(kind, size):
            return jnp.concatenate(
                [
                    column_hot(columns[:, kind * parts + p : kind * parts + p + 1], size)
                    for p in range(parts)
                ],
                axis=0,
            )

        edge_rows = rows_ref[...]
        pre = dot(edge_rows, w1_ref[0])
        pre = pre + dot(gather_hot(0, send_ref.shape[0]), send_ref[...])
        pre = pre + dot(gather_hot(1, recv_ref.shape[0]), recv_ref[...])
        pre = pre + dot(gather_hot(2, bias_ref.shape[0]), bias_ref[...])
        center, scale = center_scale(dot(silu_low(pre), w2_ref[...]))
        slot = step * rows + lax.broadcasted_iota(jnp.int32, (rows, 1), 0)
        scale = jnp.where(slot < count, scale, 0.0)
        message = (center * scale * gain_ref[...]).astype(jnp.bfloat16)
        out_ref[...] = (edge_rows.astype(jnp.float32) + message.astype(jnp.float32)).astype(
            jnp.bfloat16
        )
        spread_hot = jnp.concatenate(
            [
                row_hot(ids[parts + p : parts + p + 1, :], recv_ref.shape[0])
                for p in range(parts)
            ],
            axis=1,
        )
        total[...] += dot(spread_hot, message)

    @pl.when(step == pl.num_programs(0) - 1)
    def _():
        sum_ref[...] = total[...].astype(jnp.bfloat16)


def node_kernel(
    parts_ref, nodes_ref, w1_ref, w2_ref, gain_ref, dec_w1_ref, picks_ref, out_ref, picked_ref
):
    low = jnp.sum(parts_ref[...].astype(jnp.float32), axis=0).astype(jnp.bfloat16)
    nodes = nodes_ref[...]
    pre = dot(nodes, w1_ref[0]) + dot(low, w1_ref[1])
    center, scale = center_scale(dot(silu_low(pre), w2_ref[...]))
    fresh = (nodes.astype(jnp.float32) + center * scale * gain_ref[...]).astype(jnp.bfloat16)
    out_ref[...] = fresh
    projected = dot(fresh, dec_w1_ref[1]).astype(jnp.bfloat16)
    columns = jnp.transpose(picks_ref[...])
    for p in range(picks_ref.shape[0]):
        hot = column_hot(columns[:, p : p + 1], nodes.shape[0])
        picked_ref[p * LANES : (p + 1) * LANES, :] = dot(hot, projected).astype(jnp.bfloat16)


def decode_kernel(ids_ref, grid_ref, table_ref, w1_ref, w2_ref, gain_ref, out_ref):
    cells = grid_ref.shape[0]
    parts = cells // LANES
    fan = ids_ref.shape[1] // parts
    grid = grid_ref[...]
    shared = dot(grid, w1_ref[0])
    columns = jnp.transpose(ids_ref[0])
    message = jnp.zeros(grid.shape, jnp.float32)
    for e in range(fan):
        hot = jnp.concatenate(
            [
                column_hot(columns[:, e * parts + p : e * parts + p + 1], table_ref.shape[0])
                for p in range(parts)
            ],
            axis=0,
        )
        pre = shared + dot(hot, table_ref[...])
        center, scale = center_scale(dot(silu_low(pre), w2_ref[...]))
        message = message + center * scale
    out_ref[...] = (grid.astype(jnp.float32) + message * gain_ref[...]).astype(jnp.bfloat16)


def whole(array):
    return pl.BlockSpec(array.shape, lambda *_: (0,) * array.ndim, pipeline_mode=pl.Buffered(1))


def params():
    return pltpu.CompilerParams(vmem_limit_bytes=VMEM_BYTES)


def on_device(
    nodes,
    edges,
    senders,
    receivers,
    levels,
    counts,
    edge_w1,
    level_bias,
    edge_w2,
    edge_gain,
    node_w1,
    node_w2,
    node_gain,
    grid,
    send_rows,
    dec_index,
    dec_w1,
    dec_w2,
    dec_gain,
):
    bf16, f32 = jnp.bfloat16, jnp.float32
    block, width = nodes.shape
    row_size, col_size = lax.axis_size("row"), lax.axis_size("col")
    slots = edges.shape[2]
    peers, per_peer = send_rows.shape[1:]
    cells, fan = dec_index.shape

    send_copies, recv_copies = pl.pallas_call(
        project_kernel,
        out_shape=(
            jax.ShapeDtypeStruct((row_size, block, width), bf16),
            jax.ShapeDtypeStruct((col_size, block, width), bf16),
        ),
        compiler_params=params(),
    )(nodes, edge_w1)
    send_table = lax.all_to_all(send_copies, "row", 0, 0, tiled=True).reshape(-1, width)
    recv_table = lax.all_to_all(recv_copies, "col", 0, 0, tiled=True).reshape(-1, width)

    steps = slots // EDGE_ROWS
    edge_ids = jnp.concatenate(
        [
            ids.reshape(steps, EDGE_ROWS // LANES, LANES)
            for ids in (senders, receivers, levels)
        ],
        axis=1,
    )
    edge_ids = jnp.pad(edge_ids, ((0, 0), (0, -edge_ids.shape[1] % 8), (0, 0)))
    bias = jnp.pad(level_bias, ((0, -level_bias.shape[0] % 16), (0, 0)))
    gain = edge_gain.reshape(1, width)
    edges_out, partial_sum = pl.pallas_call(
        edge_kernel,
        grid_spec=pltpu.PrefetchScalarGridSpec(
            num_scalar_prefetch=1,
            grid=(steps,),
            in_specs=[
                pl.BlockSpec((1,) + edge_ids.shape[1:], lambda i, _: (i, 0, 0)),
                pl.BlockSpec((EDGE_ROWS, width), lambda i, _: (i, 0)),
                whole(send_table),
                whole(recv_table),
                pl.BlockSpec((1, width, width), lambda *_: (0, 0, 0), pipeline_mode=pl.Buffered(1)),
                whole(bias),
                whole(edge_w2),
                whole(gain),
            ],
            out_specs=(
                pl.BlockSpec((EDGE_ROWS, width), lambda i, _: (i, 0)),
                pl.BlockSpec(recv_table.shape, lambda *_: (0, 0)),
            ),
            scratch_shapes=[pltpu.VMEM(recv_table.shape, f32)],
        ),
        out_shape=(
            jax.ShapeDtypeStruct((slots, width), bf16),
            jax.ShapeDtypeStruct(recv_table.shape, bf16),
        ),
        compiler_params=params(),
    )(
        counts,
        edge_ids,
        edges.reshape(slots, width),
        send_table,
        recv_table,
        edge_w1,
        bias,
        edge_w2,
        gain,
    )

    node_parts = lax.all_to_all(
        partial_sum.reshape(col_size, block, width), "col", 0, 0, tiled=True
    )
    nodes_out, picked = pl.pallas_call(
        node_kernel,
        out_shape=(
            jax.ShapeDtypeStruct((block, width), bf16),
            jax.ShapeDtypeStruct((peers * per_peer, width), bf16),
        ),
        compiler_params=params(),
    )(
        node_parts,
        nodes,
        node_w1,
        node_w2,
        node_gain.reshape(1, width),
        dec_w1,
        send_rows.reshape(-1, LANES),
    )

    table = lax.all_to_all(
        picked.reshape(peers, per_peer, width), ("row", "col"), 0, 0, tiled=True
    ).reshape(-1, width)
    dec_steps = cells // CELL_ROWS
    dec_parts = CELL_ROWS // LANES
    dec_ids = (
        dec_index.T.reshape(fan, dec_steps, dec_parts, LANES)
        .transpose(1, 0, 2, 3)
        .reshape(dec_steps, fan * dec_parts, LANES)
    )
    dec_scale = dec_gain.reshape(1, width)
    grid_out = pl.pallas_call(
        decode_kernel,
        grid=(dec_steps,),
        in_specs=[
            pl.BlockSpec((1,) + dec_ids.shape[1:], lambda i: (i, 0, 0)),
            pl.BlockSpec((CELL_ROWS, width), lambda i: (i, 0)),
            whole(table),
            pl.BlockSpec((1, width, width), lambda *_: (0, 0, 0), pipeline_mode=pl.Buffered(1)),
            whole(dec_w2),
            whole(dec_scale),
        ],
        out_specs=pl.BlockSpec((CELL_ROWS, width), lambda i: (i, 0)),
        out_shape=jax.ShapeDtypeStruct((cells, width), bf16),
        compiler_params=params(),
    )(dec_ids, grid, table, dec_w1, dec_w2, dec_scale)
    return (nodes_out, edges_out.reshape(edges.shape), grid_out)


def solution(mesh):
    tile = P("row", "col", None)
    split = P(("row", "col"), None)
    return jax.shard_map(
        on_device,
        mesh=mesh,
        in_specs=(
            split,
            P("row", "col", None, None),
            tile,
            tile,
            tile,
            P("row", "col"),
            P(),
            P(),
            P(),
            P(),
            P(),
            P(),
            P(),
            split,
            P(("row", "col"), None, None),
            split,
            P(),
            P(),
            P(),
        ),
        out_specs=(split, P("row", "col", None, None), split),
        check_vma=False,
    )
```

time: 347 us -> 126 us (0.36)
  waiting for transfers between devices: 124 us -> 40.4 us
  matrix products: 83.5 us -> 0 us
  local copies, waits for them, and re-layouts: 66.4 us -> 7.51 us
  other arithmetic: 31.3 us -> 0.02 us
  Pallas kernels: 0 us -> 29.3 us
  starting transfers between devices: 8.92 us -> 31.5 us
  between operations: 14.9 us -> 1.41 us
    psum x1 -> x0, waiting for transfers between devices: 86.1 us -> none  [on_device(): lax.psum(partial_value.astype(jnp.bfloat16), 'col').astype(jnp.float32)]
    dot_general x27 -> x0, matrix products: 83.5 us -> none  [the longest x10 22.4 us: select_low(): jnp.dot(table_hot, table, preferred_element_type=jnp.float32)]
    pallas_call x0 -> x4, Pallas kernels: none -> 29.3 us  [the longest x1 13.1 us: on_device(): pl.pallas_call(edge_kernel, grid_spec=pltpu.PrefetchScalarGridSpec(num_sc...]
    all_to_all x1 -> x3, waiting for transfers between devices: 11.3 us -> 40.4 us  [the longest x1 13.9 us: on_device(): lax.all_to_all(partial_sum.reshape(col_size, block, width), 'col', 0, 0,...]
    all_gather x1 -> x0, waiting for transfers between devices: 26.4 us -> none  [on_device(): receiver_block = lax.all_gather(nodes, 'col', axis=0, tiled=True)]
    all_to_all x1 -> x3, starting transfers between devices: 8.84 us -> 31.5 us  [the longest x1 16.8 us: on_device(): lax.all_to_all(partial_sum.reshape(col_size, block, width), 'col', 0, 0,...]
    reshape x4 -> x6, local copies, waits for them, and re-layouts: 23.1 us -> 4.19 us  [the longest x1 1.96 us: on_device(): picked.reshape(peers, per_peer, width)]
    all_to_all x0 -> x1, blocking collectives: none -> 15.3 us  [on_device(): lax.all_to_all(send_copies, 'row', 0, 0, tiled=True).reshape(-1, width)]
where the time goes in v1:
time: 126 us; the launch traced here: 125 us
  waiting for transfers between devices  40.4 us (32%)
  starting transfers between devices  31.5 us (25%)
  Pallas kernels  29.3 us (23%)
  blocking collectives  15.3 us (12%)
  local copies, waits for them, and re-layouts  7.51 us (6%)
  between operations  1.41 us (1%)
    all_to_all x1, starting transfers between devices, on_device(): lax.all_to_all(partial_sum.reshape(col_size, block, width), 'col', 0, 0,...  16.8 us
    all_to_all x1, blocking collectives, on_device(): lax.all_to_all(send_copies, 'row', 0, 0, tiled=True).reshape(-1, width)  15.3 us
    all_to_all x1, waiting for transfers between devices, on_device(): lax.all_to_all(partial_sum.reshape(col_size, block, width), 'col', 0, 0,...  13.9 us
    all_to_all x1, waiting for transfers between devices, on_device(): lax.all_to_all(recv_copies, 'col', 0, 0, tiled=True).reshape(-1, width)  13.3 us
    all_to_all x1, waiting for transfers between devices, on_device(): lax.all_to_all(picked.reshape(peers, per_peer, width), ('row', 'col'), 0,...  13.2 us
    pallas_call x1, Pallas kernels, on_device(): pl.pallas_call(edge_kernel, grid_spec=pltpu.PrefetchScalarGridSpec(num_sc...  13.1 us
    pallas_call x1, Pallas kernels, on_device(): pl.pallas_call(decode_kernel, grid=(dec_steps,), in_specs=[pl.BlockSpec((...  9.34 us
    all_to_all x1, starting transfers between devices, on_device(): lax.all_to_all(recv_copies, 'col', 0, 0, tiled=True).reshape(-1, width)  7.77 us
  transfers between devices with their start and end apart: 3, of which 3 were waited for; matrix products, arithmetic and copies ran while one was open for 2% of the time, Pallas kernels for 0%

profile of v1, /device:TPU:1, one launch (start us, length us, event | category | flops | bytes accessed | tf_op | source)
XLA Modules:
  0.0 125.4 jit_solution(10048771700985573698)
XLA Ops:
  0.7 2.8 %shard_map.202 = (bf16[8,64,512]{2,1,0:T(8,128)(2,1)}, bf16[16,64,512]{2,1,0:T(8,128)(2,1)}) custom-call(bf16[64,512]{1,0:T(8,128)(2,1)} %nodes_ref.3, bf16[3,512,512]{2,1,0:T(8,128)(2,1)} %w1_ref.3), custom_call_target="tpu_custom_call" | custom-call | tf_op jit(solution)/shard_map/pallas_call | solution.py:193
  3.5 15.3 %all_to_all.20 = bf16[8,64,512]{2,1,0:T(8,128)(2,1)} all-to-all(bf16[8,64,512]{2,1,0:T(8,128)(2,1)} %get-tuple-element.9), channel_id=1, replica_groups=mesh['row'=8,'col'=16] {'row'}, dimensions={0} | all-to-all | bytes 1048576 | tf_op jit(solution)/shard_map/all_to_all | solution.py:201
  18.8 7.8 %all-to-all-start.1 = ((bf16[16,64,512]{2,1,0:T(8,128)(2,1)}), bf16[16,64,512]{2,1,0:T(8,128)(2,1)S(1)}, u32[]{:S(2)}, u32[]{:S(2)}) async-start(bf16[16,64,512]{2,1,0:T(8,128)(2,1)} %get-tuple-element.10), calls=%async_computation.1 | async-start | bytes 2097152 | tf_op jit(solution)/shard_map/all_to_all | solution.py:202
  27.2 0.0 copy-done.4
  27.2 0.0 copy-done.3
  27.2 0.0 copy-done.2
  27.3 0.6 pad.8.ids_ref
  27.9 0.0 copy-done.6
  27.9 0.6 pad.9.bias_ref
  28.5 13.3 %all-to-all-done.1 = bf16[16,64,512]{2,1,0:T(8,128)(2,1)S(1)} async-done(((bf16[16,64,512]{2,1,0:T(8,128)(2,1)}), bf16[16,64,512]{2,1,0:T(8,128)(2,1)S(1)}, u32[]{:S(2)}, u32[]{:S(2)}) %all-to-all-start.1) | async-done | bytes 1048608 | tf_op jit(solution)/shard_map/all_to_all | solution.py:202
  41.8 1.0 copy-done
  42.8 13.1 %shard_map.203 = (bf16[4096,512]{1,0:T(8,128)(2,1)}, bf16[1024,512]{1,0:T(8,128)(2,1)}) custom-call(s32[1,1]{1,0:T(1,128)S(6)} %copy.27.count_ref, s32[8,16,128]{2,1,0:T(8,128)} %pad.8.ids_ref, bf16[4096,512]{1,0:T(8,128)(2,1)} %bitcast.16, bf16[512,512]{1,0:T(8,128)(2,1)} %bitcast.17, bf16[1024,512]{1,0:T(8,128)(2,1)} %bitcast.15, ...), custom_call_target="tpu_custom_call" | custom-call | tf_op jit(solution)/shard_map/pallas_call | solution.py:215
  55.8 16.8 %all-to-all-start.2 = ((bf16[16,64,512]{2,1,0:T(8,128)(2,1)}), bf16[16,64,512]{2,1,0:T(8,128)(2,1)S(1)}, u32[]{:S(2)}, u32[]{:S(2)}) async-start(bf16[16,64,512]{2,1,0:T(8,128)(2,1)} %bitcast.18), calls=%async_computation.2 | async-start | bytes 2097152 | tf_op jit(solution)/shard_map/all_to_all | solution.py:253
  72.7 0.1 copy.24
  72.8 0.7 reshape.63.picks_ref
  73.5 13.9 %all-to-all-done.2.parts_ref = bf16[16,64,512]{2,1,0:T(8,128)(2,1)S(1)} async-done(((bf16[16,64,512]{2,1,0:T(8,128)(2,1)}), bf16[16,64,512]{2,1,0:T(8,128)(2,1)S(1)}, u32[]{:S(2)}, u32[]{:S(2)}) %all-to-all-start.2) | async-done | bytes 1048608 | tf_op jit(solution)/shard_map/all_to_all | solution.py:253
  87.4 1.0 copy-done.1
  88.4 4.0 %shard_map.204 = (bf16[64,512]{1,0:T(8,128)(2,1)}, bf16[512,512]{1,0:T(8,128)(2,1)}) custom-call(bf16[16,64,512]{2,1,0:T(8,128)(2,1)} %copy-done.1, bf16[64,512]{1,0:T(8,128)(2,1)} %nodes_ref.3, bf16[2,512,512]{2,1,0:T(8,128)(2,1)} %w1_ref.4, bf16[512,512]{1,0:T(8,128)(2,1)} %w2_ref.4, f32[1,512]{1,0:T(1,128)} %bitcast.25, bf16[2,512,512]{2,1,0:T(8,128)(2,1)} %w1_ref.5, ...), custom_call_target="tpu_custom_call" | custom-call | tf_op jit(solution)/shard_map/pallas_call | solution.py:256
  92.4 2.0 %reshape.67 = bf16[128,4,512]{2,1,0:T(4,128)(2,1)} reshape(bf16[512,512]{1,0:T(8,128)(2,1)} %get-tuple-element.14) | data formatting | bytes 1048576 | tf_op jit(solution)/shard_map/reshape | solution.py:274
  94.3 7.0 %all-to-all-start.3 = ((bf16[128,4,512]{2,1,0:T(4,128)(2,1)}), bf16[128,4,512]{2,1,0:T(4,128)(2,1)S(1)}, u32[]{:S(2)}, u32[]{:S(2)}) async-start(bf16[128,4,512]{2,1,0:T(4,128)(2,1)} %reshape.67), calls=%async_computation.3 | async-start | bytes 1048576 | tf_op jit(solution)/shard_map/all_to_all | solution.py:273
  101.3 0.6 copy.26.ids_ref
  101.9 13.2 %all-to-all-done.3 = bf16[128,4,512]{2,1,0:T(4,128)(2,1)S(1)} async-done(((bf16[128,4,512]{2,1,0:T(4,128)(2,1)}), bf16[128,4,512]{2,1,0:T(4,128)(2,1)S(1)}, u32[]{:S(2)}, u32[]{:S(2)}) %all-to-all-start.3) | async-done | bytes 524320 | tf_op jit(solution)/shard_map/all_to_all | solution.py:273
  115.2 0.9 reshape.68.table_ref
  116.1 9.3 %shard_map.205 = bf16[1024,512]{1,0:T(8,128)(2,1)} custom-call(s32[4,6,128]{2,1,0:T(8,128)} %copy.26.ids_ref, bf16[1024,512]{1,0:T(8,128)(2,1)} %grid_ref.1, bf16[512,512]{1,0:T(8,128)(2,1)} %reshape.68.table_ref, bf16[2,512,512]{2,1,0:T(8,128)(2,1)} %w1_ref.5, bf16[512,512]{1,0:T(8,128)(2,1)} %w2_ref.5, f32[1,512]{1,0:T(1,128)} %bitcast.26), custom_call_target="tpu_custom_call" | custom-call | tf_op jit(solution)/shard_map/pallas_call | solution.py:284
  (13 shorter events, 0.1 us)
Async XLA Ops:
  0.6 26.6 %copy-start.4 = (s32[1,1,4096]{2,1,0:T(1,128)S(1)}, s32[1,1,4096]{2,1,0:T(1,128)}, u32[]{:S(2)}) copy-start(s32[1,1,4096]{2,1,0:T(1,128)} %param.21) | copy-start | bytes 49156
  0.6 26.6 %copy-start.3 = (s32[1,1,4096]{2,1,0:T(1,128)S(1)}, s32[1,1,4096]{2,1,0:T(1,128)}, u32[]{:S(2)}) copy-start(s32[1,1,4096]{2,1,0:T(1,128)} %param.22) | copy-start | bytes 49156
  0.7 26.6 %copy-start.2 = (s32[1,1,4096]{2,1,0:T(1,128)S(1)}, s32[1,1,4096]{2,1,0:T(1,128)}, u32[]{:S(2)}) copy-start(s32[1,1,4096]{2,1,0:T(1,128)} %param.23) | copy-start | bytes 49156
  0.7 27.2 %copy-start.6 = (bf16[7,512]{1,0:T(8,128)(2,1)S(1)}, bf16[7,512]{1,0:T(8,128)(2,1)}, u32[]{:S(2)}) copy-start(bf16[7,512]{1,0:T(8,128)(2,1)} %param.26) | copy-start | bytes 21508
  18.8 23.0 %all-to-all-start.1 = ((bf16[16,64,512]{2,1,0:T(8,128)(2,1)}), bf16[16,64,512]{2,1,0:T(8,128)(2,1)S(1)}, u32[]{:S(2)}, u32[]{:S(2)}) async-start(bf16[16,64,512]{2,1,0:T(8,128)(2,1)} %get-tuple-element.10), calls=%async_computation.1 | async-start | bytes 2097152 | tf_op jit(solution)/shard_map/all_to_all | solution.py:202
  41.8 1.0 copy-start
  42.8 29.9 %copy-start.7 = (s32[1,128,4]{1,2,0:T(4,128)S(1)}, s32[1,128,4]{1,2,0:T(4,128)}, u32[]{:S(2)}) copy-start(s32[1,128,4]{1,2,0:T(4,128)} %param.33) | copy-start | bytes 6148
  55.8 45.5 %copy-start.5 = (s32[1024,3]{0,1:T(4,128)S(1)}, s32[1024,3]{0,1:T(4,128)}, u32[]{:S(2)}) copy-start(s32[1024,3]{0,1:T(4,128)} %param.34) | copy-start | bytes 36868
  55.8 31.6 %all-to-all-start.2 = ((bf16[16,64,512]{2,1,0:T(8,128)(2,1)}), bf16[16,64,512]{2,1,0:T(8,128)(2,1)S(1)}, u32[]{:S(2)}, u32[]{:S(2)}) async-start(bf16[16,64,512]{2,1,0:T(8,128)(2,1)} %bitcast.18), calls=%async_computation.2 | async-start | bytes 2097152 | tf_op jit(solution)/shard_map/all_to_all | solution.py:253
  87.4 1.0 copy-start.1
  94.3 20.8 %all-to-all-start.3 = ((bf16[128,4,512]{2,1,0:T(4,128)(2,1)}), bf16[128,4,512]{2,1,0:T(4,128)(2,1)S(1)}, u32[]{:S(2)}, u32[]{:S(2)}) async-start(bf16[128,4,512]{2,1,0:T(4,128)(2,1)} %reshape.67), calls=%async_computation.3 | async-start | bytes 1048576 | tf_op jit(solution)/shard_map/all_to_all | solution.py:273

commit v2 on v1

v2 whole, which is shorter than its diff:
```python
import jax
import jax.numpy as jnp
from jax import lax
from jax.experimental import pallas as pl
from jax.experimental.pallas import tpu as pltpu
from jax.sharding import PartitionSpec as P

EPSILON = 1e-05
LANES = 128
EDGE_ROWS = 1024
CHUNK = 256
CELL_ROWS = 256


def dot(a, b):
    return jnp.dot(a, b, preferred_element_type=jnp.float32)


def silu_half(half):
    return (half + half * jnp.tanh(half)).astype(jnp.bfloat16)


def center_scale(values):
    center = values - jnp.mean(values, axis=-1, keepdims=True)
    spread = jnp.mean(center * center, axis=-1, keepdims=True)
    return center, lax.rsqrt(spread + EPSILON)


def column_hot(ids, count):
    lanes = lax.broadcasted_iota(jnp.int32, (ids.shape[0], count), 1)
    return (ids == lanes).astype(jnp.bfloat16)


def stacked_hot(columns, first, number, count):
    return jnp.concatenate(
        [column_hot(columns[:, p : p + 1], count) for p in range(first, first + number)], axis=0
    )


def row_hot(ids, count):
    rows = lax.broadcasted_iota(jnp.int32, (count, ids.shape[1]), 0)
    return (ids == rows).astype(jnp.bfloat16)


def project_kernel(nodes_ref, send_weight_ref, recv_weight_ref, send_ref, recv_ref):
    nodes = nodes_ref[...]
    recv = (0.5 * dot(nodes, recv_weight_ref[0])).astype(jnp.bfloat16)
    for k in range(recv_ref.shape[0]):
        recv_ref[k] = recv
    send_ref[...] = (0.5 * dot(nodes, send_weight_ref[0])).astype(jnp.bfloat16)


def edge_first_kernel(ids_ref, rows_ref, w1_ref, bias_ref, half_ref):
    columns = jnp.transpose(ids_ref[0])
    levels = bias_ref.shape[0]
    for p in range(rows_ref.shape[0] // CHUNK):
        part = slice(p * CHUNK, (p + 1) * CHUNK)
        hot = stacked_hot(columns, p * CHUNK // LANES, CHUNK // LANES, levels)
        half_ref[part, :] = 0.5 * (dot(rows_ref[part, :], w1_ref[0]) + dot(hot, bias_ref[...]))


def grid_first_kernel(grid_ref, w1_ref, half_ref):
    half_ref[...] = 0.5 * dot(grid_ref[...], w1_ref[0])


def edge_kernel(
    place_ref,
    ids_ref,
    rows_ref,
    half_ref,
    near_ref,
    far1_ref,
    far2_ref,
    far3_ref,
    recv_ref,
    w2_ref,
    gain_ref,
    out_ref,
    sum_ref,
    total,
    table,
    messages,
):
    step = pl.program_id(0)
    rows = rows_ref.shape[0]
    parts = rows // LANES
    count, chip = place_ref[0], place_ref[1]
    send_count = table.shape[0] - recv_ref.shape[0]

    @pl.when(step == 0)
    def _():
        total[...] = jnp.zeros_like(total)
        sources = (near_ref, far1_ref, far2_ref, far3_ref)
        span = near_ref.shape[0]
        for k, source in enumerate(sources):
            owner = lax.rem(chip - k + len(sources), len(sources))
            table[pl.ds(pl.multiple_of(owner * span, span), span), :] = source[...]
        table[send_count:, :] = recv_ref[...]

    @pl.when(step * rows >= count)
    def _():
        out_ref[...] = rows_ref[...]

    @pl.when(step * rows < count)
    def _():
        ids = ids_ref[0]
        columns = jnp.transpose(ids)

        def first(c):
            hot = jnp.concatenate(
                [
                    stacked_hot(columns, c * CHUNK // LANES, CHUNK // LANES, send_count),
                    stacked_hot(
                        columns, parts + c * CHUNK // LANES, CHUNK // LANES, recv_ref.shape[0]
                    ),
                ],
                axis=1,
            )
            return silu_half(half_ref[c * CHUNK : (c + 1) * CHUNK, :] + dot(hot, table[...]))

        def second(c, hidden):
            part = slice(c * CHUNK, (c + 1) * CHUNK)
            center, scale = center_scale(dot(hidden, w2_ref[...]))
            slot = step * rows + c * CHUNK + lax.broadcasted_iota(jnp.int32, (CHUNK, 1), 0)
            scale = jnp.where(slot < count, scale, 0.0)
            message = (center * scale * gain_ref[...]).astype(jnp.bfloat16)
            out_ref[part, :] = (
                rows_ref[part, :].astype(jnp.float32) + message.astype(jnp.float32)
            ).astype(jnp.bfloat16)
            messages[part, :] = message

        hidden = first(0)
        for c in range(rows // CHUNK):
            later = first(c + 1) if (c + 1) * CHUNK < rows else None
            second(c, hidden)
            hidden = later
        spread_hot = jnp.concatenate(
            [
                row_hot(ids[parts + p : parts + p + 1, :], recv_ref.shape[0])
                for p in range(parts)
            ],
            axis=1,
        )
        total[...] += dot(spread_hot, messages[...])

    @pl.when(step == pl.num_programs(0) - 1)
    def _():
        sum_ref[...] = total[...].astype(jnp.bfloat16)


def node_kernel(
    parts_ref, nodes_ref, w1_ref, w2_ref, gain_ref, dec_w1_ref, picks_ref, out_ref, picked_ref, wide
):
    low = jnp.sum(parts_ref[...].astype(jnp.float32), axis=0).astype(jnp.bfloat16)
    nodes = nodes_ref[...]
    pre = dot(nodes, w1_ref[0]) + dot(low, w1_ref[1])
    center, scale = center_scale(dot(silu_half(0.5 * pre), w2_ref[...]))
    fresh = (nodes.astype(jnp.float32) + center * scale * gain_ref[...]).astype(jnp.bfloat16)
    out_ref[...] = fresh
    projected = (0.5 * dot(fresh, dec_w1_ref[0])).astype(jnp.bfloat16)
    peers, strips, _ = picked_ref.shape
    columns = jnp.transpose(picks_ref[...])
    groups = strips // picks_ref.shape[0]
    for j in range(picks_ref.shape[0]):
        chosen = dot(column_hot(columns[:, j : j + 1], nodes.shape[0]), projected)
        for q in range(groups):
            wide[pl.ds(j * groups + q, peers, stride=strips), :] = chosen[
                :, q * LANES : (q + 1) * LANES
            ]
    picked_ref[...] = wide[...].reshape(picked_ref.shape).astype(jnp.bfloat16)


def decode_kernel(
    ids_ref, grid_ref, half_ref, received_ref, w2_ref, gain_ref, out_ref, wide, table
):
    cells = grid_ref.shape[0]
    parts = cells // LANES
    fan = ids_ref.shape[1] // parts
    peers, strips, _ = received_ref.shape
    groups = table.shape[1] // LANES
    per_peer = strips // groups

    @pl.when(pl.program_id(0) == 0)
    def _():
        wide[...] = received_ref[...].astype(jnp.float32).reshape(wide.shape)
        for j in range(per_peer):
            for q in range(groups):
                table[j * peers : (j + 1) * peers, q * LANES : (q + 1) * LANES] = wide[
                    pl.ds(j * groups + q, peers, stride=strips), :
                ].astype(jnp.bfloat16)

    ids = ids_ref[0]
    columns = jnp.transpose(lax.rem(ids, per_peer) * peers + lax.div(ids, per_peer))
    shared = half_ref[...]

    def first(e):
        hot = stacked_hot(columns, e * parts, parts, table.shape[0])
        return silu_half(shared + dot(hot, table[...]))

    message = jnp.zeros(grid_ref.shape, jnp.float32)
    hidden = first(0)
    for e in range(fan):
        later = first(e + 1) if e + 1 < fan else None
        center, scale = center_scale(dot(hidden, w2_ref[...]))
        message = message + center * scale
        hidden = later
    out_ref[...] = (grid_ref[...].astype(jnp.float32) + message * gain_ref[...]).astype(
        jnp.bfloat16
    )


def whole(array):
    return pl.BlockSpec(array.shape, lambda *_: (0,) * array.ndim, pipeline_mode=pl.Buffered(1))


def layer(k, width):
    return pl.BlockSpec((1, width, width), lambda *_: (k, 0, 0), pipeline_mode=pl.Buffered(1))


def params(mib):
    return pltpu.CompilerParams(vmem_limit_bytes=mib * 1024 * 1024)


def on_device(
    nodes,
    edges,
    senders,
    receivers,
    levels,
    counts,
    edge_w1,
    level_bias,
    edge_w2,
    edge_gain,
    node_w1,
    node_w2,
    node_gain,
    grid,
    send_rows,
    dec_index,
    dec_w1,
    dec_w2,
    dec_gain,
):
    bf16, f32 = jnp.bfloat16, jnp.float32
    block, width = nodes.shape
    row_size, col_size = lax.axis_size("row"), lax.axis_size("col")
    slots = edges.shape[2]
    peers, per_peer = send_rows.shape[1:]
    cells, fan = dec_index.shape
    recv_count = block * col_size
    rows = edges.reshape(slots, width)

    send_own, recv_copies = pl.pallas_call(
        project_kernel,
        grid=(1,),
        in_specs=[whole(nodes), layer(1, width), layer(2, width)],
        out_specs=(
            pl.BlockSpec((block, width), lambda i: (0, 0)),
            pl.BlockSpec((col_size, block, width), lambda i: (0, 0, 0)),
        ),
        out_shape=(
            jax.ShapeDtypeStruct((block, width), bf16),
            jax.ShapeDtypeStruct((col_size, block, width), bf16),
        ),
        compiler_params=params(57),
        name="project",
    )(nodes, edge_w1, edge_w1)
    recv_table = lax.all_to_all(recv_copies, "col", 0, 0, tiled=True).reshape(-1, width)
    own = lax.axis_index("row")
    send_pair = lax.ppermute(send_own, "row", [(i, i ^ 1) for i in range(row_size)])
    near = jnp.where(
        own % 2 == 0,
        jnp.concatenate([send_own, send_pair]),
        jnp.concatenate([send_pair, send_own]),
    )
    rows_first, grid_rows, near = lax.optimization_barrier((rows, grid, near))
    far = [
        lax.ppermute(near, "row", [(i, (i + 2 * k) % row_size) for i in range(row_size)])
        for k in range(1, row_size // 2)
    ]
    steps = slots // EDGE_ROWS
    parts = EDGE_ROWS // LANES
    level_ids = levels.reshape(steps, parts, LANES)
    edge_half = pl.pallas_call(
        edge_first_kernel,
        grid=(steps,),
        in_specs=[
            pl.BlockSpec((1, parts, LANES), lambda i: (i, 0, 0)),
            pl.BlockSpec((EDGE_ROWS, width), lambda i: (i, 0)),
            layer(0, width),
            whole(level_bias),
        ],
        out_specs=pl.BlockSpec((EDGE_ROWS, width), lambda i: (i, 0)),
        out_shape=jax.ShapeDtypeStruct((slots, width), f32),
        compiler_params=params(57),
        cost_estimate=pl.CostEstimate(
            flops=2 * slots * width * width, bytes_accessed=6 * slots * width, transcendentals=0
        ),
        name="edge_first",
    )(level_ids, rows_first, edge_w1, level_bias)
    grid_half = pl.pallas_call(
        grid_first_kernel,
        grid=(cells // CELL_ROWS,),
        in_specs=[pl.BlockSpec((CELL_ROWS, width), lambda i: (i, 0)), layer(0, width)],
        out_specs=pl.BlockSpec((CELL_ROWS, width), lambda i: (i, 0)),
        out_shape=jax.ShapeDtypeStruct((cells, width), f32),
        compiler_params=params(57),
        cost_estimate=pl.CostEstimate(
            flops=2 * cells * width * width, bytes_accessed=6 * cells * width, transcendentals=0
        ),
        name="grid_first",
    )(grid_rows, dec_w1)

    edge_ids = jnp.concatenate(
        [ids.reshape(steps, parts, LANES) for ids in (senders, receivers)], axis=1
    )
    place = jnp.stack([counts[0, 0], own // 2])
    gain = edge_gain.reshape(1, width)
    block_spec = pl.BlockSpec((EDGE_ROWS, width), lambda i, _: (i, 0))
    edges_out, partial_sum = pl.pallas_call(
        edge_kernel,
        grid_spec=pltpu.PrefetchScalarGridSpec(
            num_scalar_prefetch=1,
            grid=(steps,),
            in_specs=[
                pl.BlockSpec((1, 2 * parts, LANES), lambda i, _: (i, 0, 0)),
                block_spec,
                block_spec,
                whole(near),
                *(whole(rows_far) for rows_far in far),
                whole(recv_table),
                whole(edge_w2),
                whole(gain),
            ],
            out_specs=(block_spec, pl.BlockSpec((recv_count, width), lambda *_: (0, 0))),
            scratch_shapes=[
                pltpu.VMEM((recv_count, width), f32),
                pltpu.VMEM((block * row_size + recv_count, width), bf16),
                pltpu.VMEM((EDGE_ROWS, width), bf16),
            ],
        ),
        out_shape=(
            jax.ShapeDtypeStruct((slots, width), bf16),
            jax.ShapeDtypeStruct((recv_count, width), bf16),
        ),
        compiler_params=params(50),
        name="edges",
    )(place, edge_ids, rows, edge_half, near, *far, recv_table, edge_w2, gain)

    node_parts = lax.all_to_all(
        partial_sum.reshape(col_size, block, width), "col", 0, 0, tiled=True
    )
    strips = per_peer * width // LANES
    picks = send_rows[0].T
    node_scale = node_gain.reshape(1, width)
    nodes_out, picked = pl.pallas_call(
        node_kernel,
        grid=(1,),
        in_specs=[
            whole(node_parts),
            whole(nodes),
            whole(node_w1),
            whole(node_w2),
            whole(node_scale),
            layer(1, width),
            whole(picks),
        ],
        out_specs=(
            pl.BlockSpec((block, width), lambda i: (0, 0)),
            pl.BlockSpec((peers, strips, LANES), lambda i: (0, 0, 0)),
        ),
        out_shape=(
            jax.ShapeDtypeStruct((block, width), bf16),
            jax.ShapeDtypeStruct((peers, strips, LANES), bf16),
        ),
        scratch_shapes=[pltpu.VMEM((peers * strips, LANES), f32)],
        compiler_params=params(12),
        name="nodes",
    )(node_parts, nodes, node_w1, node_w2, node_scale, dec_w1, picks)

    received = lax.all_to_all(picked, ("row", "col"), 0, 0, tiled=True)
    dec_steps = cells // CELL_ROWS
    dec_parts = CELL_ROWS // LANES
    dec_ids = (
        dec_index.T.reshape(fan, dec_steps, dec_parts, LANES)
        .transpose(1, 0, 2, 3)
        .reshape(dec_steps, fan * dec_parts, LANES)
    )
    dec_scale = dec_gain.reshape(1, width)
    cell_spec = pl.BlockSpec((CELL_ROWS, width), lambda i: (i, 0))
    grid_out = pl.pallas_call(
        decode_kernel,
        grid=(dec_steps,),
        in_specs=[
            pl.BlockSpec((1, fan * dec_parts, LANES), lambda i: (i, 0, 0)),
            cell_spec,
            cell_spec,
            whole(received),
            whole(dec_w2),
            whole(dec_scale),
        ],
        out_specs=cell_spec,
        out_shape=jax.ShapeDtypeStruct((cells, width), bf16),
        scratch_shapes=[
            pltpu.VMEM((peers * strips, LANES), f32),
            pltpu.VMEM((peers * per_peer, width), bf16),
        ],
        compiler_params=params(52),
        name="decoder",
    )(dec_ids, grid, grid_half, received, dec_w2, dec_scale)
    return (nodes_out, edges_out.reshape(edges.shape), grid_out)


def solution(mesh):
    tile = P("row", "col", None)
    split = P(("row", "col"), None)
    return jax.shard_map(
        on_device,
        mesh=mesh,
        in_specs=(
            split,
            P("row", "col", None, None),
            tile,
            tile,
            tile,
            P("row", "col"),
            P(),
            P(),
            P(),
            P(),
            P(),
            P(),
            P(),
            split,
            P(("row", "col"), None, None),
            split,
            P(),
            P(),
            P(),
        ),
        out_specs=(split, P("row", "col", None, None), split),
        check_vma=False,
    )
```

time: 126 us -> 100 us (0.79)
  waiting for transfers between devices: 40.4 us -> 9.99 us
  blocking collectives: 15.3 us -> 27.6 us
  starting transfers between devices: 31.5 us -> 19.9 us
  Pallas kernels: 29.3 us -> 39.6 us
  local copies, waits for them, and re-layouts: 7.51 us -> 0.1 us
    all_to_all x2 -> x1, starting transfers between devices: 23.8 us -> 5.33 us  [on_device(): received = lax.all_to_all(picked, ('row', 'col'), 0, 0, tiled=True)]
    all_to_all x2 -> x1, waiting for transfers between devices: 27.1 us -> 9.63 us  [on_device(): received = lax.all_to_all(picked, ('row', 'col'), 0, 0, tiled=True)]
    all_to_all x1, waiting for transfers between devices: 13.3 us -> 0.01 us  [on_device(): lax.all_to_all(recv_copies, 'col', 0, 0, tiled=True).reshape(-1, width)]
    all_to_all x1, blocking collectives: 15.3 us -> 27.6 us  [on_device(): lax.all_to_all(partial_sum.reshape(col_size, block, width), 'col', 0, 0,...]
    pallas_call x2 -> x4, Pallas kernels: 6.85 us -> 17.2 us  [the longest x1 8.22 us: on_device(): pl.pallas_call(edge_first_kernel, grid=(steps,), in_specs=[pl.BlockSpec((...]
    ppermute x0 -> x4, starting transfers between devices: none -> 5.92 us  [the longest x3 4.88 us: on_device(): lax.ppermute(near, 'row', [(i, (i + 2 * k) % row_size) for i in range(row...]
    reshape x3 -> x0, local copies, waits for them, and re-layouts: 3.57 us -> none  [the longest x1 1.96 us: on_device(): picked.reshape(peers, per_peer, width)]
    unnamed x17 -> x26, local copies, waits for them, and re-layouts: 2.08 us -> 0.07 us
  transfers between devices with their start and end apart: 3 -> 6, of which waited for: 3 -> 2; matrix products, arithmetic and copies ran while one was open for 2% -> 1% of each run, Pallas kernels for 0% -> 13%
where the time goes in v2:
time: 100 us; the launch traced here: 99.7 us
  Pallas kernels  39.6 us (40%)
  blocking collectives  27.6 us (28%)
  starting transfers between devices  19.9 us (20%)
  waiting for transfers between devices  9.99 us (10%)
  between operations  1.5 us (2%)
  other arithmetic  1.03 us (1%)
    all_to_all x1, blocking collectives, on_device(): lax.all_to_all(partial_sum.reshape(col_size, block, width), 'col', 0, 0,...  27.6 us
    pallas_call x1, Pallas kernels, on_device(): pl.pallas_call(edge_kernel, grid_spec=pltpu.PrefetchScalarGridSpec(num_sc...  14.4 us
    all_to_all x1, waiting for transfers between devices, on_device(): received = lax.all_to_all(picked, ('row', 'col'), 0, 0, tiled=True)  9.63 us
    all_to_all x1, starting transfers between devices, on_device(): lax.all_to_all(recv_copies, 'col', 0, 0, tiled=True).reshape(-1, width)  8.6 us
    pallas_call x1, Pallas kernels, on_device(): pl.pallas_call(edge_first_kernel, grid=(steps,), in_specs=[pl.BlockSpec((...  8.22 us
    pallas_call x1, Pallas kernels, on_device(): pl.pallas_call(decode_kernel, grid=(dec_steps,), in_specs=[pl.BlockSpec((...  7.92 us
    all_to_all x1, starting transfers between devices, on_device(): received = lax.all_to_all(picked, ('row', 'col'), 0, 0, tiled=True)  5.33 us
    ppermute x3, starting transfers between devices, on_device(): lax.ppermute(near, 'row', [(i, (i + 2 * k) % row_size) for i in range(row...  4.88 us
  transfers between devices with their start and end apart: 6, of which 2 were waited for; matrix products, arithmetic and copies ran while one was open for 1% of the time, Pallas kernels for 13%

profile of v2, /device:TPU:1, one launch (start us, length us, event | category | flops | bytes accessed | tf_op | source)
XLA Modules:
  0.0 99.7 jit_solution(15874142146713363355)
XLA Ops:
  0.7 2.5 %project.1 = (bf16[64,512]{1,0:T(8,128)(2,1)}, bf16[16,64,512]{2,1,0:T(8,128)(2,1)}) custom-call(bf16[64,512]{1,0:T(8,128)(2,1)} %nodes_ref.3, bf16[3,512,512]{2,1,0:T(8,128)(2,1)} %w1_ref.3, bf16[3,512,512]{2,1,0:T(8,128)(2,1)} %w1_ref.3), custom_call_target="tpu_custom_call" | custom-call | tf_op jit(solution)/shard_map/project/pallas_call | solution.py:254
  3.2 8.6 %all-to-all-start = ((bf16[16,64,512]{2,1,0:T(8,128)(2,1)}), bf16[16,64,512]{2,1,0:T(8,128)(2,1)S(1)}, u32[]{:S(2)}, u32[]{:S(2)}) async-start(bf16[16,64,512]{2,1,0:T(8,128)(2,1)} %get-tuple-element.15), calls=%async_computation | async-start | bytes 2097152 | tf_op jit(solution)/shard_map/all_to_all | solution.py:269
  11.8 1.0 %collective-permute-start = (bf16[64,512]{1,0:T(8,128)(2,1)}, bf16[64,512]{1,0:T(8,128)(2,1)S(1)}, u32[]{:S(2)}, u32[]{:S(2)}) collective-permute-start(bf16[64,512]{1,0:T(8,128)(2,1)} %get-tuple-element.12), channel_id=1, source_target_pairs={{0,16},{16,0},{32,48},{48,32},{64,80},{80,64},{96,112},{112,96},{1... | collective-permute-start | bytes 196616 | tf_op jit(solution)/shard_map/ppermute | solution.py:271
  13.5 0.1 pad_add_fusion.1.place_ref
  13.6 0.3 collective-permute-done
  13.9 0.9 maximum_select_fusion.near_ref
  14.9 1.3 %collective-permute-start.1 = (bf16[128,512]{1,0:T(8,128)(2,1)S(1)}, bf16[128,512]{1,0:T(8,128)(2,1)S(1)}, u32[]{:S(2)}, u32[]{:S(2)}) collective-permute-start(bf16[128,512]{1,0:T(8,128)(2,1)S(1)} %maximum_select_fusion.near_ref), channel_id=1, source_target_pairs={{0,32},{16,48},{32,64},{48,80},{64,96},{80,112},{96,0},{112,16},{1... | collective-permute-start | bytes 393224 | tf_op jit(solution)/shard_map/ppermute | solution.py:279
  16.1 2.4 %collective-permute-start.2 = (bf16[128,512]{1,0:T(8,128)(2,1)S(1)}, bf16[128,512]{1,0:T(8,128)(2,1)S(1)}, u32[]{:S(2)}, u32[]{:S(2)}) collective-permute-start(bf16[128,512]{1,0:T(8,128)(2,1)S(1)} %maximum_select_fusion.near_ref), channel_id=1, source_target_pairs={{0,64},{16,80},{32,96},{48,112},{64,0},{80,16},{96,32},{112,48},{1... | collective-permute-start | bytes 393224 | tf_op jit(solution)/shard_map/ppermute | solution.py:279
  18.6 1.2 %collective-permute-start.3 = (bf16[128,512]{1,0:T(8,128)(2,1)S(1)}, bf16[128,512]{1,0:T(8,128)(2,1)S(1)}, u32[]{:S(2)}, u32[]{:S(2)}) collective-permute-start(bf16[128,512]{1,0:T(8,128)(2,1)S(1)} %maximum_select_fusion.near_ref), channel_id=1, source_target_pairs={{0,96},{16,112},{32,0},{48,16},{64,32},{80,48},{96,64},{112,80},{1... | collective-permute-start | bytes 393224 | tf_op jit(solution)/shard_map/ppermute | solution.py:279
  19.7 8.2 %edge_first.1.half_ref = f32[4096,512]{1,0:T(8,128)} custom-call(s32[4,8,128]{2,1,0:T(8,128)} %bitcast.32, bf16[4096,512]{1,0:T(8,128)(2,1)} %bitcast.26, bf16[3,512,512]{2,1,0:T(8,128)(2,1)} %w1_ref.3, bf16[7,512]{1,0:T(8,128)(2,1)} %bias_ref.1), custom_call_target="tpu_custom_call" | custom-call | flops 2147483648 | bytes 12582912 | tf_op jit(solution)/shard_map/edge_first/pallas_call | solution.py:285
  28.0 0.0 copy-start
  28.0 0.0 copy-start.1
  28.0 0.0 copy-start.4
  28.1 0.0 copy-start.5
  28.1 0.0 copy-start.7
  28.1 0.0 copy-start.8
  28.1 14.4 %edges.1 = (bf16[4096,512]{1,0:T(8,128)(2,1)}, bf16[1024,512]{1,0:T(8,128)(2,1)S(1)}) custom-call(s32[2]{0:T(128)S(1)} %pad_add_fusion.1.place_ref, s32[4,16,128]{2,1,0:T(8,128)S(1)} %pad_add_fusion.ids_ref, bf16[4096,512]{1,0:T(8,128)(2,1)} %bitcast.27, f32[4096,512]{1,0:T(8,128)} %edge_first.1.half_ref, bf16[128,512]{1,0:T(8,128)(2,1)S(1)} %maximum_select_fusion.near_ref, ...), custom_call_target="tpu_custom_call" | custom-call | tf_op jit(solution)/shard_map/edges/pallas_call | solution.py:321
  42.5 27.6 %all_to_all.15.parts_ref = bf16[16,64,512]{2,1,0:T(8,128)(2,1)S(1)} all-to-all(bf16[16,64,512]{2,1,0:T(8,128)(2,1)S(1)} %bitcast.21), channel_id=1, replica_groups=mesh['row'=8,'col'=16] {'col'}, dimensions={0} | all-to-all | bytes 2097152 | tf_op jit(solution)/shard_map/all_to_all | solution.py:351
  70.2 0.0 copy-start.9
  70.2 2.1 %nodes.1 = (bf16[64,512]{1,0:T(8,128)(2,1)}, bf16[128,16,128]{2,1,0:T(8,128)(2,1)}) custom-call(bf16[16,64,512]{2,1,0:T(8,128)(2,1)S(1)} %all_to_all.15.parts_ref, bf16[64,512]{1,0:T(8,128)(2,1)S(1)} %copy-done.5, bf16[2,512,512]{2,1,0:T(8,128)(2,1)S(1)} %copy-done.1, bf16[512,512]{1,0:T(8,128)(2,1)S(1)} %copy-done.4, f32[1,512]{1,0:T(1,128)S(1)} %bitcast.23, ...), custom_call_target="tpu_custom_call" | custom-call | tf_op jit(solution)/shard_map/nodes/pallas_call | solution.py:357
  72.4 5.3 %all-to-all-start.2 = ((bf16[128,16,128]{2,1,0:T(8,128)(2,1)}), bf16[128,16,128]{2,1,0:T(8,128)(2,1)S(1)}, u32[]{:S(2)}, u32[]{:S(2)}) async-start(bf16[128,16,128]{2,1,0:T(8,128)(2,1)} %get-tuple-element.20), calls=%async_computation.2 | async-start | bytes 1048576 | tf_op jit(solution)/shard_map/all_to_all | solution.py:382
  77.8 4.3 %grid_first.1.half_ref = f32[1024,512]{1,0:T(8,128)} custom-call(bf16[1024,512]{1,0:T(8,128)(2,1)} %grid_ref.2, bf16[2,512,512]{2,1,0:T(8,128)(2,1)} %w1_ref.5), custom_call_target="tpu_custom_call" | custom-call | flops 536870912 | bytes 3145728 | tf_op jit(solution)/shard_map/grid_first/pallas_call | solution.py:302
  82.1 9.6 %all-to-all-done.2.received_ref = bf16[128,16,128]{2,1,0:T(8,128)(2,1)S(1)} async-done(((bf16[128,16,128]{2,1,0:T(8,128)(2,1)}), bf16[128,16,128]{2,1,0:T(8,128)(2,1)S(1)}, u32[]{:S(2)}, u32[]{:S(2)}) %all-to-all-start.2) | async-done | bytes 524320 | tf_op jit(solution)/shard_map/all_to_all | solution.py:382
  91.8 7.9 %decoder.1 = bf16[1024,512]{1,0:T(8,128)(2,1)} custom-call(s32[4,6,128]{2,1,0:T(8,128)S(1)} %copy.24.ids_ref, bf16[1024,512]{1,0:T(8,128)(2,1)} %grid_ref.2, f32[1024,512]{1,0:T(8,128)} %grid_first.1.half_ref, bf16[128,16,128]{2,1,0:T(8,128)(2,1)S(1)} %all-to-all-done.2.received_ref, bf16[512,512]{1,0:T(8,128)(2,1)S(1)} %copy-done.3, f32[1,512]{1,0:T(1,128)S(1)} %bitcast.25), custom_call_target="tpu_custom_call" | custom-call | tf_op jit(solution)/shard_map/decoder/pallas_call | solution.py:392
  (27 shorter events, 0.1 us)
Async XLA Ops:
  0.6 12.8 %copy-start.12 = (s32[1,1,4096]{2,1,0:T(1,128)S(1)}, s32[1,1,4096]{2,1,0:T(1,128)}, u32[]{:S(2)}) copy-start(s32[1,1,4096]{2,1,0:T(1,128)} %param.21) | copy-start | bytes 49156
  0.6 12.8 %copy-start.11 = (s32[1,1,4096]{2,1,0:T(1,128)S(1)}, s32[1,1,4096]{2,1,0:T(1,128)}, u32[]{:S(2)}) copy-start(s32[1,1,4096]{2,1,0:T(1,128)} %param.22) | copy-start | bytes 49156
  3.2 24.8 %all-to-all-start = ((bf16[16,64,512]{2,1,0:T(8,128)(2,1)}), bf16[16,64,512]{2,1,0:T(8,128)(2,1)S(1)}, u32[]{:S(2)}, u32[]{:S(2)}) async-start(bf16[16,64,512]{2,1,0:T(8,128)(2,1)} %get-tuple-element.15), calls=%async_computation | async-start | bytes 2097152 | tf_op jit(solution)/shard_map/all_to_all | solution.py:269
  11.8 2.1 %collective-permute-start = (bf16[64,512]{1,0:T(8,128)(2,1)}, bf16[64,512]{1,0:T(8,128)(2,1)S(1)}, u32[]{:S(2)}, u32[]{:S(2)}) collective-permute-start(bf16[64,512]{1,0:T(8,128)(2,1)} %get-tuple-element.12), channel_id=1, source_target_pairs={{0,16},{16,0},{32,48},{48,32},{64,80},{80,64},{96,112},{112,96},{1... | collective-permute-start | bytes 196616 | tf_op jit(solution)/shard_map/ppermute | solution.py:271
  14.9 13.1 %collective-permute-start.1 = (bf16[128,512]{1,0:T(8,128)(2,1)S(1)}, bf16[128,512]{1,0:T(8,128)(2,1)S(1)}, u32[]{:S(2)}, u32[]{:S(2)}) collective-permute-start(bf16[128,512]{1,0:T(8,128)(2,1)S(1)} %maximum_select_fusion.near_ref), channel_id=1, source_target_pairs={{0,32},{16,48},{32,64},{48,80},{64,96},{80,112},{96,0},{112,16},{1... | collective-permute-start | bytes 393224 | tf_op jit(solution)/shard_map/ppermute | solution.py:279
  16.1 11.8 %collective-permute-start.2 = (bf16[128,512]{1,0:T(8,128)(2,1)S(1)}, bf16[128,512]{1,0:T(8,128)(2,1)S(1)}, u32[]{:S(2)}, u32[]{:S(2)}) collective-permute-start(bf16[128,512]{1,0:T(8,128)(2,1)S(1)} %maximum_select_fusion.near_ref), channel_id=1, source_target_pairs={{0,64},{16,80},{32,96},{48,112},{64,0},{80,16},{96,32},{112,48},{1... | collective-permute-start | bytes 393224 | tf_op jit(solution)/shard_map/ppermute | solution.py:279
  18.6 9.4 %collective-permute-start.3 = (bf16[128,512]{1,0:T(8,128)(2,1)S(1)}, bf16[128,512]{1,0:T(8,128)(2,1)S(1)}, u32[]{:S(2)}, u32[]{:S(2)}) collective-permute-start(bf16[128,512]{1,0:T(8,128)(2,1)S(1)} %maximum_select_fusion.near_ref), channel_id=1, source_target_pairs={{0,96},{16,112},{32,0},{48,16},{64,32},{80,48},{96,64},{112,80},{1... | collective-permute-start | bytes 393224 | tf_op jit(solution)/shard_map/ppermute | solution.py:279
  19.7 8.3 %copy-start.2 = (bf16[512,512]{1,0:T(8,128)(2,1)S(1)}, bf16[512,512]{1,0:T(8,128)(2,1)}, u32[]{:S(2)}) copy-start(bf16[512,512]{1,0:T(8,128)(2,1)} %w2_ref.3) | copy-start | bytes 1572868
  19.7 8.3 %copy-start.6 = (f32[512]{0:T(512)S(1)}, f32[512]{0:T(512)}, u32[]{:S(2)}) copy-start(f32[512]{0:T(512)} %param.28) | copy-start | bytes 6148
  28.0 42.2 %copy-start = (bf16[2,512,512]{2,1,0:T(8,128)(2,1)S(1)}, bf16[2,512,512]{2,1,0:T(8,128)(2,1)}, u32[]{:S(2)}) copy-start(bf16[2,512,512]{2,1,0:T(8,128)(2,1)} %w1_ref.5) | copy-start | bytes 3145732
  28.0 42.1 %copy-start.1 = (bf16[2,512,512]{2,1,0:T(8,128)(2,1)S(1)}, bf16[2,512,512]{2,1,0:T(8,128)(2,1)}, u32[]{:S(2)}) copy-start(bf16[2,512,512]{2,1,0:T(8,128)(2,1)} %w1_ref.4) | copy-start | bytes 3145732
  28.0 42.1 %copy-start.4 = (bf16[512,512]{1,0:T(8,128)(2,1)S(1)}, bf16[512,512]{1,0:T(8,128)(2,1)}, u32[]{:S(2)}) copy-start(bf16[512,512]{1,0:T(8,128)(2,1)} %w2_ref.4) | copy-start | bytes 1572868
  28.1 42.1 %copy-start.5 = (bf16[64,512]{1,0:T(8,128)(2,1)S(1)}, bf16[64,512]{1,0:T(8,128)(2,1)}, u32[]{:S(2)}) copy-start(bf16[64,512]{1,0:T(8,128)(2,1)} %nodes_ref.3) | copy-start | bytes 196612
  28.1 42.1 %copy-start.7 = (f32[512]{0:T(512)S(1)}, f32[512]{0:T(512)}, u32[]{:S(2)}) copy-start(f32[512]{0:T(512)} %param.31) | copy-start | bytes 6148
  28.1 42.1 %copy-start.8 = (s32[1,128,4]{1,2,0:T(4,128)S(1)}, s32[1,128,4]{1,2,0:T(4,128)}, u32[]{:S(2)}) copy-start(s32[1,128,4]{1,2,0:T(4,128)} %param.33) | copy-start | bytes 6148
  42.5 35.2 %copy-start.10 = (s32[1024,3]{0,1:T(4,128)S(1)}, s32[1024,3]{0,1:T(4,128)}, u32[]{:S(2)}) copy-start(s32[1024,3]{0,1:T(4,128)} %param.34) | copy-start | bytes 36868
  70.2 21.5 %copy-start.3 = (bf16[512,512]{1,0:T(8,128)(2,1)S(1)}, bf16[512,512]{1,0:T(8,128)(2,1)}, u32[]{:S(2)}) copy-start(bf16[512,512]{1,0:T(8,128)(2,1)} %w2_ref.5) | copy-start | bytes 1572868
  70.2 21.5 %copy-start.9 = (f32[512]{0:T(512)S(1)}, f32[512]{0:T(512)}, u32[]{:S(2)}) copy-start(f32[512]{0:T(512)} %param.37) | copy-start | bytes 6148
  72.4 19.4 %all-to-all-start.2 = ((bf16[128,16,128]{2,1,0:T(8,128)(2,1)}), bf16[128,16,128]{2,1,0:T(8,128)(2,1)S(1)}, u32[]{:S(2)}, u32[]{:S(2)}) async-start(bf16[128,16,128]{2,1,0:T(8,128)(2,1)} %get-tuple-element.20), calls=%async_computation.2 | async-start | bytes 1048576 | tf_op jit(solution)/shard_map/all_to_all | solution.py:382

commit v3 on v2

v3 whole, which is shorter than its diff:
```python
import jax
import jax.numpy as jnp
from jax import lax
from jax.experimental import pallas as pl
from jax.experimental.pallas import tpu as pltpu
from jax.sharding import PartitionSpec as P

EPSILON = 1e-05
LANES = 128
EDGE_ROWS = 1024
CHUNK = 256
AHEAD = 2


def dot(a, b):
    return jnp.dot(a, b, preferred_element_type=jnp.float32)


def silu_half(half):
    return (half + half * jnp.tanh(half)).astype(jnp.bfloat16)


def center_scale(values):
    center = values - jnp.mean(values, axis=-1, keepdims=True)
    spread = jnp.mean(center * center, axis=-1, keepdims=True)
    return center, lax.rsqrt(spread + EPSILON)


def column_hot(ids, count):
    lanes = lax.broadcasted_iota(jnp.int32, (ids.shape[0], count), 1)
    return (ids == lanes).astype(jnp.bfloat16)


def stacked_hot(columns, first, number, count):
    return jnp.concatenate(
        [column_hot(columns[:, p : p + 1], count) for p in range(first, first + number)], axis=0
    )


def row_hot(ids, count):
    rows = lax.broadcasted_iota(jnp.int32, (count, ids.shape[1]), 0)
    return (ids == rows).astype(jnp.bfloat16)


def project_kernel(nodes_ref, send_weight_ref, recv_weight_ref, send_ref, recv_ref):
    nodes = nodes_ref[...]
    recv = (0.5 * dot(nodes, recv_weight_ref[0])).astype(jnp.bfloat16)
    for k in range(recv_ref.shape[0]):
        recv_ref[k] = recv
    send_ref[...] = (0.5 * dot(nodes, send_weight_ref[0])).astype(jnp.bfloat16)


def edge_first_kernel(
    ids_ref, rows_ref, w1_ref, bias_ref, half_ref, rows, half, weight, row_sems, half_sems, weight_sem
):
    blocks = ids_ref.shape[0]
    span = ids_ref.shape[1] * LANES
    weight_copy = pltpu.make_async_copy(w1_ref.at[0], weight, weight_sem)
    weight_copy.start()
    copies = [
        pltpu.make_async_copy(
            rows_ref.at[pl.ds(k * span, span)], rows.at[pl.ds(k * span, span)], row_sems.at[k]
        )
        for k in range(blocks)
    ]
    for copy in copies[:AHEAD]:
        copy.start()
    weight_copy.wait()
    outs = []
    for k in range(blocks):
        columns = jnp.transpose(ids_ref[k])
        hot = stacked_hot(columns, 0, ids_ref.shape[1], bias_ref.shape[0])
        copies[k].wait()
        if k + AHEAD < blocks:
            copies[k + AHEAD].start()
        part = slice(k * span, (k + 1) * span)
        product = dot(rows[part, :], weight[...]) + dot(hot, bias_ref[...])
        half[part, :] = (0.5 * product).astype(jnp.bfloat16)
        place = pl.ds(k * span, span)
        outs.append(pltpu.make_async_copy(half.at[place], half_ref.at[place], half_sems.at[k]))
        outs[-1].start()
    for out in outs:
        out.wait()


def edge_kernel(
    place_ref,
    ids_ref,
    rows_ref,
    half_ref,
    near_ref,
    far1_ref,
    far2_ref,
    far3_ref,
    recv_ref,
    w2_ref,
    gain_ref,
    out_ref,
    sum_ref,
    total,
    table,
    messages,
    edge_rows,
    half,
    row_sems,
    half_sems,
    out_sems,
):
    blocks = ids_ref.shape[0]
    parts = ids_ref.shape[1] // 2
    rows = parts * LANES
    count, chip = place_ref[0], place_ref[1]
    send_count = table.shape[0] - recv_ref.shape[0]

    def stream(source, target, sems, k):
        place = pl.ds(pl.multiple_of(k * rows, rows), rows)
        return pltpu.make_async_copy(source.at[place], target.at[place], sems.at[k])

    for k in range(blocks):
        stream(half_ref, half, half_sems, k).start()
        stream(rows_ref, edge_rows, row_sems, k).start()
    total[...] = jnp.zeros_like(total)
    sources = (near_ref, far1_ref, far2_ref, far3_ref)
    span = near_ref.shape[0]
    for k, source in enumerate(sources):
        owner = lax.rem(chip - k + len(sources), len(sources))
        table[pl.ds(pl.multiple_of(owner * span, span), span), :] = source[...]
    table[send_count:, :] = recv_ref[...]

    @pl.loop(0, blocks)
    def _(step):
        base = pl.multiple_of(step * rows, rows)

        stream(half_ref, half, half_sems, step).wait()
        stream(rows_ref, edge_rows, row_sems, step).wait()

        @pl.when(base >= count)
        def _():
            stream(edge_rows, out_ref, out_sems, step).start()

        @pl.when(base < count)
        def _():
            ids = ids_ref[step]
            columns = jnp.transpose(ids)

            def first(c):
                hot = jnp.concatenate(
                    [
                        stacked_hot(columns, c * CHUNK // LANES, CHUNK // LANES, send_count),
                        stacked_hot(
                            columns, parts + c * CHUNK // LANES, CHUNK // LANES, recv_ref.shape[0]
                        ),
                    ],
                    axis=1,
                )
                known = half[pl.ds(base + c * CHUNK, CHUNK), :].astype(jnp.float32)
                return silu_half(known + dot(hot, table[...]))

            def second(c, hidden):
                center, scale = center_scale(dot(hidden, w2_ref[...]))
                slot = base + c * CHUNK + lax.broadcasted_iota(jnp.int32, (CHUNK, 1), 0)
                scale = jnp.where(slot < count, scale, 0.0)
                message = (center * scale * gain_ref[...]).astype(jnp.bfloat16)
                messages[c * CHUNK : (c + 1) * CHUNK, :] = message
                place = pl.ds(base + c * CHUNK, CHUNK)
                edge_rows[place, :] = (
                    edge_rows[place, :].astype(jnp.float32) + message.astype(jnp.float32)
                ).astype(jnp.bfloat16)

            hidden = first(0)
            for c in range(rows // CHUNK):
                later = first(c + 1) if (c + 1) * CHUNK < rows else None
                second(c, hidden)
                hidden = later
            stream(edge_rows, out_ref, out_sems, step).start()
            spread_hot = jnp.concatenate(
                [
                    row_hot(ids[parts + p : parts + p + 1, :], recv_ref.shape[0])
                    for p in range(parts)
                ],
                axis=1,
            )
            total[...] += dot(spread_hot, messages[...])

    sum_ref[...] = total[...].astype(jnp.bfloat16)
    for k in range(blocks):
        stream(edge_rows, out_ref, out_sems, k).wait()


def grid_first_kernel(ids_ref, grid_ref, w1_ref, half_ref, hot_ref):
    cells = grid_ref.shape[0]
    half_ref[...] = (0.5 * dot(grid_ref[...], w1_ref[0])).astype(jnp.bfloat16)
    per_peer = hot_ref.shape[1] // LANES
    ids = ids_ref[...]
    columns = jnp.transpose(lax.rem(ids, per_peer) * LANES + lax.div(ids, per_peer))
    parts = CHUNK // LANES
    fan = hot_ref.shape[0] // cells
    for b in range(cells // CHUNK):
        for e in range(fan):
            start = (b * fan + e) * CHUNK
            hot_ref[start : start + CHUNK, :] = stacked_hot(
                columns, e * (cells // LANES) + b * parts, parts, hot_ref.shape[1]
            )


def node_kernel(
    parts_ref, nodes_ref, w1_ref, w2_ref, gain_ref, dec_w1_ref, picks_ref, out_ref, picked_ref, wide
):
    low = jnp.sum(parts_ref[...].astype(jnp.float32), axis=0).astype(jnp.bfloat16)
    nodes = nodes_ref[...]
    pre = dot(nodes, w1_ref[0]) + dot(low, w1_ref[1])
    center, scale = center_scale(dot(silu_half(0.5 * pre), w2_ref[...]))
    fresh = (nodes.astype(jnp.float32) + center * scale * gain_ref[...]).astype(jnp.bfloat16)
    out_ref[...] = fresh
    projected = (0.5 * dot(fresh, dec_w1_ref[0])).astype(jnp.bfloat16)
    peers, strips, _ = picked_ref.shape
    columns = jnp.transpose(picks_ref[...])
    groups = strips // picks_ref.shape[0]
    for j in range(picks_ref.shape[0]):
        chosen = dot(column_hot(columns[:, j : j + 1], nodes.shape[0]), projected)
        for q in range(groups):
            wide[pl.ds(j * groups + q, peers, stride=strips), :] = chosen[
                :, q * LANES : (q + 1) * LANES
            ]
    picked_ref[...] = wide[...].reshape(picked_ref.shape).astype(jnp.bfloat16)


def decode_kernel(
    hot_ref,
    grid_ref,
    half_ref,
    received_ref,
    w2_ref,
    gain_ref,
    out_ref,
    received,
    w2,
    hot,
    half,
    grid,
    wide,
    table,
    result,
    sems,
    hot_sems,
    half_sems,
    out_sems,
):
    cells = grid_ref.shape[0]
    blocks = cells // CHUNK
    fan = hot_ref.shape[0] // cells
    peers, strips, _ = received_ref.shape
    groups = table.shape[1] // LANES

    def stream(source, target, sems, k, rows):
        place = pl.ds(k * rows, rows)
        return pltpu.make_async_copy(source.at[place], target.at[place], sems.at[k])

    received_copy = pltpu.make_async_copy(received_ref, received, sems.at[0])
    w2_copy = pltpu.make_async_copy(w2_ref, w2, sems.at[1])
    grid_copy = pltpu.make_async_copy(grid_ref, grid, sems.at[2])
    def fetch(b):
        stream(hot_ref, hot, hot_sems, b, fan * CHUNK).start()
        stream(half_ref, half, half_sems, b, CHUNK).start()

    received_copy.start()
    fetch(0)
    w2_copy.start()
    received_copy.wait()
    wide[...] = received[...].astype(jnp.float32).reshape(wide.shape)
    for j in range(strips // groups):
        for q in range(groups):
            table[j * peers : (j + 1) * peers, q * LANES : (q + 1) * LANES] = wide[
                pl.ds(j * groups + q, peers, stride=strips), :
            ].astype(jnp.bfloat16)

    def first(b, e):
        if e == 0:
            stream(hot_ref, hot, hot_sems, b, fan * CHUNK).wait()
            stream(half_ref, half, half_sems, b, CHUNK).wait()
            if b == 0:
                grid_copy.start()
            if b + 1 < blocks:
                fetch(b + 1)
        rows = pl.ds((b * fan + e) * CHUNK, CHUNK)
        known = half[b * CHUNK : (b + 1) * CHUNK, :].astype(jnp.float32)
        return silu_half(known + dot(hot[rows, :], table[...]))

    work = [(b, e) for b in range(blocks) for e in range(fan)]
    hidden = first(*work[0])
    w2_copy.wait()
    for k, (b, e) in enumerate(work):
        later = first(*work[k + 1]) if k + 1 < len(work) else None
        center, scale = center_scale(dot(hidden, w2[...]))
        message = center * scale if e == 0 else message + center * scale
        hidden = later
        if e == fan - 1:
            if b == 0:
                grid_copy.wait()
            part = pl.ds(b * CHUNK, CHUNK)
            result[part, :] = (
                grid[part, :].astype(jnp.float32) + message * gain_ref[...]
            ).astype(jnp.bfloat16)
            stream(result, out_ref, out_sems, b, CHUNK).start()
    for b in range(blocks):
        stream(result, out_ref, out_sems, b, CHUNK).wait()


def whole(array):
    return pl.BlockSpec(array.shape, lambda *_: (0,) * array.ndim, pipeline_mode=pl.Buffered(1))


def layer(k, width):
    return pl.BlockSpec((1, width, width), lambda *_: (k, 0, 0), pipeline_mode=pl.Buffered(1))


def params(mib):
    return pltpu.CompilerParams(vmem_limit_bytes=mib * 1024 * 1024)


def on_device(
    nodes,
    edges,
    senders,
    receivers,
    levels,
    counts,
    edge_w1,
    level_bias,
    edge_w2,
    edge_gain,
    node_w1,
    node_w2,
    node_gain,
    grid,
    send_rows,
    dec_index,
    dec_w1,
    dec_w2,
    dec_gain,
):
    bf16, f32 = jnp.bfloat16, jnp.float32
    block, width = nodes.shape
    row_size, col_size = lax.axis_size("row"), lax.axis_size("col")
    slots = edges.shape[2]
    peers, per_peer = send_rows.shape[1:]
    cells, fan = dec_index.shape
    recv_count = block * col_size
    rows = edges.reshape(slots, width)

    send_own, recv_copies = pl.pallas_call(
        project_kernel,
        grid=(1,),
        in_specs=[whole(nodes), layer(1, width), layer(2, width)],
        out_specs=(
            pl.BlockSpec((block, width), lambda i: (0, 0)),
            pl.BlockSpec((col_size, block, width), lambda i: (0, 0, 0)),
        ),
        out_shape=(
            jax.ShapeDtypeStruct((block, width), bf16),
            jax.ShapeDtypeStruct((col_size, block, width), bf16),
        ),
        compiler_params=params(57),
        name="project",
    )(nodes, edge_w1, edge_w1)
    recv_table = lax.all_to_all(recv_copies, "col", 0, 0, tiled=True).reshape(-1, width)
    own = lax.axis_index("row")
    send_pair = lax.ppermute(send_own, "row", [(i, i ^ 1) for i in range(row_size)])
    near = jnp.where(
        own % 2 == 0,
        jnp.concatenate([send_own, send_pair]),
        jnp.concatenate([send_pair, send_own]),
    )
    rows_first, near = lax.optimization_barrier((rows, near))
    far = [
        lax.ppermute(near, "row", [(i, (i + 2 * k) % row_size) for i in range(row_size)])
        for k in range(1, row_size // 2)
    ]
    steps = slots // EDGE_ROWS
    parts = EDGE_ROWS // LANES
    level_ids = levels.reshape(steps, parts, LANES)
    vmem, hbm = pl.BlockSpec(memory_space=pltpu.VMEM), pl.BlockSpec(memory_space=pltpu.HBM)
    edge_half = pl.pallas_call(
        edge_first_kernel,
        in_specs=[vmem, hbm, hbm, vmem],
        out_specs=hbm,
        out_shape=jax.ShapeDtypeStruct((slots, width), bf16),
        scratch_shapes=[
            pltpu.VMEM((slots, width), bf16),
            pltpu.VMEM((slots, width), bf16),
            pltpu.VMEM((width, width), bf16),
            pltpu.SemaphoreType.DMA((steps,)),
            pltpu.SemaphoreType.DMA((steps,)),
            pltpu.SemaphoreType.DMA,
        ],
        compiler_params=params(57),
        cost_estimate=pl.CostEstimate(
            flops=2 * slots * width * width, bytes_accessed=2 * slots * width, transcendentals=0
        ),
        name="edge_first",
    )(level_ids, rows_first, edge_w1, level_bias)

    edge_ids = jnp.concatenate(
        [ids.reshape(steps, parts, LANES) for ids in (senders, receivers)], axis=1
    )
    place = jnp.stack([counts[0, 0], own // 2])
    gain = edge_gain.reshape(1, width)
    smem = pl.BlockSpec(memory_space=pltpu.SMEM)
    edges_out, partial_sum = pl.pallas_call(
        edge_kernel,
        in_specs=[smem, vmem, hbm, hbm] + [vmem] * (4 + len(far)),
        out_specs=(hbm, vmem),
        out_shape=(
            jax.ShapeDtypeStruct((slots, width), bf16),
            jax.ShapeDtypeStruct((recv_count, width), bf16),
        ),
        scratch_shapes=[
            pltpu.VMEM((recv_count, width), f32),
            pltpu.VMEM((block * row_size + recv_count, width), bf16),
            pltpu.VMEM((EDGE_ROWS, width), bf16),
            pltpu.VMEM((slots, width), bf16),
            pltpu.VMEM((slots, width), bf16),
            pltpu.SemaphoreType.DMA((steps,)),
            pltpu.SemaphoreType.DMA((steps,)),
            pltpu.SemaphoreType.DMA((steps,)),
        ],
        compiler_params=params(50),
        name="edges",
    )(place, edge_ids, rows, edge_half, near, *far, recv_table, edge_w2, gain)

    node_parts = lax.all_to_all(
        partial_sum.reshape(col_size, block, width), "col", 0, 0, tiled=True
    )
    strips = per_peer * width // LANES
    picks = send_rows[0].T
    node_scale = node_gain.reshape(1, width)
    nodes_out, picked = pl.pallas_call(
        node_kernel,
        grid=(1,),
        in_specs=[
            whole(node_parts),
            whole(nodes),
            whole(node_w1),
            whole(node_w2),
            whole(node_scale),
            layer(1, width),
            whole(picks),
        ],
        out_specs=(
            pl.BlockSpec((block, width), lambda i: (0, 0)),
            pl.BlockSpec((peers, strips, LANES), lambda i: (0, 0, 0)),
        ),
        out_shape=(
            jax.ShapeDtypeStruct((block, width), bf16),
            jax.ShapeDtypeStruct((peers, strips, LANES), bf16),
        ),
        scratch_shapes=[pltpu.VMEM((peers * strips, LANES), f32)],
        compiler_params=params(12),
        name="nodes",
    )(node_parts, nodes, node_w1, node_w2, node_scale, dec_w1, picks)

    received = lax.all_to_all(picked, ("row", "col"), 0, 0, tiled=True)
    dec_scale = dec_gain.reshape(1, width)
    dec_blocks = cells // CHUNK
    grid_half, dec_hot = pl.pallas_call(
        grid_first_kernel,
        grid=(1,),
        in_specs=[pl.BlockSpec((fan * cells // LANES, LANES), lambda i: (0, 0)), whole(grid), layer(0, width)],
        out_specs=(
            pl.BlockSpec((cells, width), lambda i: (0, 0)),
            pl.BlockSpec((fan * cells, peers * per_peer), lambda i: (0, 0)),
        ),
        out_shape=(
            jax.ShapeDtypeStruct((cells, width), bf16),
            jax.ShapeDtypeStruct((fan * cells, peers * per_peer), bf16),
        ),
        compiler_params=params(57),
        cost_estimate=pl.CostEstimate(
            flops=2 * cells * width * width, bytes_accessed=6 * cells * width, transcendentals=0
        ),
        name="grid_first",
    )(dec_index.T.reshape(-1, LANES), grid, dec_w1)
    grid_out = pl.pallas_call(
        decode_kernel,
        in_specs=[hbm] * 5 + [vmem],
        out_specs=hbm,
        out_shape=jax.ShapeDtypeStruct((cells, width), bf16),
        scratch_shapes=[
            pltpu.VMEM(received.shape, bf16),
            pltpu.VMEM(dec_w2.shape, bf16),
            pltpu.VMEM(dec_hot.shape, bf16),
            pltpu.VMEM(grid_half.shape, bf16),
            pltpu.VMEM(grid.shape, bf16),
            pltpu.VMEM((peers * strips, LANES), f32),
            pltpu.VMEM((peers * per_peer, width), bf16),
            pltpu.VMEM((cells, width), bf16),
            pltpu.SemaphoreType.DMA((3,)),
            pltpu.SemaphoreType.DMA((dec_blocks,)),
            pltpu.SemaphoreType.DMA((dec_blocks,)),
            pltpu.SemaphoreType.DMA((dec_blocks,)),
        ],
        compiler_params=params(53),
        name="decoder",
    )(dec_hot, grid, grid_half, received, dec_w2, dec_scale)
    return (nodes_out, edges_out.reshape(edges.shape), grid_out)


def solution(mesh):
    tile = P("row", "col", None)
    split = P(("row", "col"), None)
    return jax.shard_map(
        on_device,
        mesh=mesh,
        in_specs=(
            split,
            P("row", "col", None, None),
            tile,
            tile,
            tile,
            P("row", "col"),
            P(),
            P(),
            P(),
            P(),
            P(),
            P(),
            P(),
            split,
            P(("row", "col"), None, None),
            split,
            P(),
            P(),
            P(),
        ),
        out_specs=(split, P("row", "col", None, None), split),
        check_vma=False,
    )
```

time: 100 us -> 97.6 us (0.976)
  Pallas kernels: 39.6 us -> 35.3 us
  blocking collectives: 27.6 us -> 28.7 us
    pallas_call x4, Pallas kernels: 34.9 us -> 30.6 us  [the longest x1 11.5 us: on_device(): pl.pallas_call(edge_kernel, in_specs=[smem, vmem, hbm, hbm] + [vmem] * (4...]
    all_to_all x1, blocking collectives: 27.6 us -> 28.7 us  [on_device(): lax.all_to_all(partial_sum.reshape(col_size, block, width), 'col', 0, 0,...]
  transfers between devices with their start and end apart: 6 -> 6, of which waited for: 2 -> 3; matrix products, arithmetic and copies ran while one was open for 1% -> 2% of each run, Pallas kernels for 13% -> 12%
where the time goes in v3:
time: 97.6 us; the launch traced here: 97.2 us
  Pallas kernels  35.3 us (36%)
  blocking collectives  28.7 us (29%)
  starting transfers between devices  20.2 us (21%)
  waiting for transfers between devices  9.66 us (10%)
  between operations  1.64 us (2%)
  other arithmetic  1.03 us (1%)
    all_to_all x1, blocking collectives, on_device(): lax.all_to_all(partial_sum.reshape(col_size, block, width), 'col', 0, 0,...  28.7 us
    pallas_call x1, Pallas kernels, on_device(): pl.pallas_call(edge_kernel, in_specs=[smem, vmem, hbm, hbm] + [vmem] * (4...  11.5 us
    all_to_all x1, waiting for transfers between devices, on_device(): received = lax.all_to_all(picked, ('row', 'col'), 0, 0, tiled=True)  9.23 us
    all_to_all x1, starting transfers between devices, on_device(): lax.all_to_all(recv_copies, 'col', 0, 0, tiled=True).reshape(-1, width)  8.6 us
    pallas_call x1, Pallas kernels, on_device(): pl.pallas_call(decode_kernel, in_specs=[hbm] * 5 + [vmem], out_specs=hbm,...  7.61 us
    pallas_call x1, Pallas kernels, on_device(): pl.pallas_call(edge_first_kernel, in_specs=[vmem, hbm, hbm, vmem], out_sp...  7.41 us
    all_to_all x1, starting transfers between devices, on_device(): received = lax.all_to_all(picked, ('row', 'col'), 0, 0, tiled=True)  5.73 us
    ppermute x3, starting transfers between devices, on_device(): lax.ppermute(near, 'row', [(i, (i + 2 * k) % row_size) for i in range(row...  4.88 us
  transfers between devices with their start and end apart: 6, of which 3 were waited for; matrix products, arithmetic and copies ran while one was open for 2% of the time, Pallas kernels for 12%

profile of v3, /device:TPU:1, one launch (start us, length us, event | category | flops | bytes accessed | tf_op | source)
XLA Modules:
  0.0 97.2 jit_solution(17222048864267249111)
XLA Ops:
  0.7 2.5 %project.1 = (bf16[64,512]{1,0:T(8,128)(2,1)}, bf16[16,64,512]{2,1,0:T(8,128)(2,1)}) custom-call(bf16[64,512]{1,0:T(8,128)(2,1)} %nodes_ref.3, bf16[3,512,512]{2,1,0:T(8,128)(2,1)} %w1_ref.3, bf16[3,512,512]{2,1,0:T(8,128)(2,1)} %w1_ref.3), custom_call_target="tpu_custom_call" | custom-call | tf_op jit(solution)/shard_map/project/pallas_call | solution.py:351
  3.2 8.6 %all-to-all-start = ((bf16[16,64,512]{2,1,0:T(8,128)(2,1)}), bf16[16,64,512]{2,1,0:T(8,128)(2,1)S(1)}, u32[]{:S(2)}, u32[]{:S(2)}) async-start(bf16[16,64,512]{2,1,0:T(8,128)(2,1)} %get-tuple-element.16), calls=%async_computation | async-start | bytes 2097152 | tf_op jit(solution)/shard_map/all_to_all | solution.py:366
  11.8 1.0 %collective-permute-start = (bf16[64,512]{1,0:T(8,128)(2,1)}, bf16[64,512]{1,0:T(8,128)(2,1)S(1)}, u32[]{:S(2)}, u32[]{:S(2)}) collective-permute-start(bf16[64,512]{1,0:T(8,128)(2,1)} %get-tuple-element.13), channel_id=1, source_target_pairs={{0,16},{16,0},{32,48},{48,32},{64,80},{80,64},{96,112},{112,96},{1... | collective-permute-start | bytes 196616 | tf_op jit(solution)/shard_map/ppermute | solution.py:368
  13.5 0.1 pad_add_fusion.1.place_ref
  13.6 0.3 collective-permute-done
  13.9 0.9 maximum_select_fusion.near_ref
  14.9 1.3 %collective-permute-start.1 = (bf16[128,512]{1,0:T(8,128)(2,1)S(1)}, bf16[128,512]{1,0:T(8,128)(2,1)S(1)}, u32[]{:S(2)}, u32[]{:S(2)}) collective-permute-start(bf16[128,512]{1,0:T(8,128)(2,1)S(1)} %maximum_select_fusion.near_ref), channel_id=1, source_target_pairs={{0,32},{16,48},{32,64},{48,80},{64,96},{80,112},{96,0},{112,16},{1... | collective-permute-start | bytes 393224 | tf_op jit(solution)/shard_map/ppermute | solution.py:376
  16.1 2.4 %collective-permute-start.2 = (bf16[128,512]{1,0:T(8,128)(2,1)S(1)}, bf16[128,512]{1,0:T(8,128)(2,1)S(1)}, u32[]{:S(2)}, u32[]{:S(2)}) collective-permute-start(bf16[128,512]{1,0:T(8,128)(2,1)S(1)} %maximum_select_fusion.near_ref), channel_id=1, source_target_pairs={{0,64},{16,80},{32,96},{48,112},{64,0},{80,16},{96,32},{112,48},{1... | collective-permute-start | bytes 393224 | tf_op jit(solution)/shard_map/ppermute | solution.py:376
  18.6 1.2 %collective-permute-start.3 = (bf16[128,512]{1,0:T(8,128)(2,1)S(1)}, bf16[128,512]{1,0:T(8,128)(2,1)S(1)}, u32[]{:S(2)}, u32[]{:S(2)}) collective-permute-start(bf16[128,512]{1,0:T(8,128)(2,1)S(1)} %maximum_select_fusion.near_ref), channel_id=1, source_target_pairs={{0,96},{16,112},{32,0},{48,16},{64,32},{80,48},{96,64},{112,80},{1... | collective-permute-start | bytes 393224 | tf_op jit(solution)/shard_map/ppermute | solution.py:376
  19.7 7.4 %edge_first.1.half_ref = bf16[4096,512]{1,0:T(8,128)(2,1)} custom-call(s32[4,8,128]{2,1,0:T(8,128)} %bitcast.25, bf16[4096,512]{1,0:T(8,128)(2,1)} %bitcast.23, bf16[3,512,512]{2,1,0:T(8,128)(2,1)} %w1_ref.3, bf16[7,512]{1,0:T(8,128)(2,1)} %bias_ref.1), custom_call_target="tpu_custom_call" | custom-call | flops 2147483648 | bytes 4194304 | tf_op jit(solution)/shard_map/edge_first/pallas_call | solution.py:383
  27.2 0.1 all-to-all-done
  27.3 0.0 copy-start.3
  27.3 0.0 copy-start.4
  27.3 0.0 copy-start.6
  27.3 0.0 copy-start.7
  27.3 11.5 %edges.1 = (bf16[4096,512]{1,0:T(8,128)(2,1)}, bf16[1024,512]{1,0:T(8,128)(2,1)S(1)}) custom-call(s32[2]{0:T(128)S(1)} %pad_add_fusion.1.place_ref, s32[4,16,128]{2,1,0:T(8,128)S(1)} %pad_add_fusion.ids_ref, bf16[4096,512]{1,0:T(8,128)(2,1)} %bitcast.24, bf16[4096,512]{1,0:T(8,128)(2,1)} %edge_first.1.half_ref, ...), custom_call_target="tpu_custom_call" | custom-call | tf_op jit(solution)/shard_map/edges/pallas_call | solution.py:409
  38.8 0.0 copy-start.9
  38.8 28.7 %all_to_all.15.parts_ref = bf16[16,64,512]{2,1,0:T(8,128)(2,1)S(1)} all-to-all(bf16[16,64,512]{2,1,0:T(8,128)(2,1)S(1)} %bitcast.18), channel_id=1, replica_groups=mesh['row'=8,'col'=16] {'col'}, dimensions={0} | all-to-all | bytes 2097152 | tf_op jit(solution)/shard_map/all_to_all | solution.py:431
  67.6 2.1 %nodes.1 = (bf16[64,512]{1,0:T(8,128)(2,1)}, bf16[128,16,128]{2,1,0:T(8,128)(2,1)}) custom-call(bf16[16,64,512]{2,1,0:T(8,128)(2,1)S(1)} %all_to_all.15.parts_ref, bf16[64,512]{1,0:T(8,128)(2,1)S(1)} %copy-done.4, bf16[2,512,512]{2,1,0:T(8,128)(2,1)S(1)} %copy-done.1, bf16[512,512]{1,0:T(8,128)(2,1)S(1)} %copy-done.3, f32[1,512]{1,0:T(1,128)S(1)} %bitcast.20, ...), custom_call_target="tpu_custom_call" | custom-call | tf_op jit(solution)/shard_map/nodes/pallas_call | solution.py:437
  69.7 5.7 %all-to-all-start.2 = ((bf16[128,16,128]{2,1,0:T(8,128)(2,1)}), bf16[128,16,128]{2,1,0:T(8,128)(2,1)S(1)}, u32[]{:S(2)}, u32[]{:S(2)}) async-start(bf16[128,16,128]{2,1,0:T(8,128)(2,1)} %get-tuple-element.22), calls=%async_computation.2 | async-start | bytes 1048576 | tf_op jit(solution)/shard_map/all_to_all | solution.py:462
  75.5 0.6 reshape.48.ids_ref
  76.1 4.2 %grid_first.1 = (bf16[1024,512]{1,0:T(8,128)(2,1)}, bf16[3072,512]{1,0:T(8,128)(2,1)}) custom-call(s32[24,128]{1,0:T(8,128)} %reshape.48.ids_ref, bf16[1024,512]{1,0:T(8,128)(2,1)} %grid_ref.3, bf16[2,512,512]{2,1,0:T(8,128)(2,1)} %w1_ref.5), custom_call_target="tpu_custom_call" | custom-call | flops 536870912 | bytes 3145728 | tf_op jit(solution)/shard_map/grid_first/pallas_call | solution.py:465
  80.2 9.2 %all-to-all-done.2.received_ref = bf16[128,16,128]{2,1,0:T(8,128)(2,1)S(1)} async-done(((bf16[128,16,128]{2,1,0:T(8,128)(2,1)}), bf16[128,16,128]{2,1,0:T(8,128)(2,1)S(1)}, u32[]{:S(2)}, u32[]{:S(2)}) %all-to-all-start.2) | async-done | bytes 524320 | tf_op jit(solution)/shard_map/all_to_all | solution.py:462
  89.5 7.6 %decoder.1 = bf16[1024,512]{1,0:T(8,128)(2,1)} custom-call(bf16[3072,512]{1,0:T(8,128)(2,1)} %get-tuple-element.20.hot_ref, bf16[1024,512]{1,0:T(8,128)(2,1)} %grid_ref.3, bf16[1024,512]{1,0:T(8,128)(2,1)} %get-tuple-element.21.half_ref, bf16[128,16,128]{2,1,0:T(8,128)(2,1)S(1)} %all-to-all-done.2.received_ref, bf16[512,512]{1,0:T(8,128)(2,1)} %w2_ref.5, ...), custom_call_target="tpu_custom_call" | custom-call | tf_op jit(solution)/shard_map/decoder/pallas_call | solution.py:483
  (23 shorter events, 0.1 us)
Async XLA Ops:
  0.6 12.8 %copy-start.11 = (s32[1,1,4096]{2,1,0:T(1,128)S(1)}, s32[1,1,4096]{2,1,0:T(1,128)}, u32[]{:S(2)}) copy-start(s32[1,1,4096]{2,1,0:T(1,128)} %param.21) | copy-start | bytes 49156
  0.6 12.8 %copy-start.10 = (s32[1,1,4096]{2,1,0:T(1,128)S(1)}, s32[1,1,4096]{2,1,0:T(1,128)}, u32[]{:S(2)}) copy-start(s32[1,1,4096]{2,1,0:T(1,128)} %param.22) | copy-start | bytes 49156
  3.2 24.1 %all-to-all-start = ((bf16[16,64,512]{2,1,0:T(8,128)(2,1)}), bf16[16,64,512]{2,1,0:T(8,128)(2,1)S(1)}, u32[]{:S(2)}, u32[]{:S(2)}) async-start(bf16[16,64,512]{2,1,0:T(8,128)(2,1)} %get-tuple-element.16), calls=%async_computation | async-start | bytes 2097152 | tf_op jit(solution)/shard_map/all_to_all | solution.py:366
  11.8 2.1 %collective-permute-start = (bf16[64,512]{1,0:T(8,128)(2,1)}, bf16[64,512]{1,0:T(8,128)(2,1)S(1)}, u32[]{:S(2)}, u32[]{:S(2)}) collective-permute-start(bf16[64,512]{1,0:T(8,128)(2,1)} %get-tuple-element.13), channel_id=1, source_target_pairs={{0,16},{16,0},{32,48},{48,32},{64,80},{80,64},{96,112},{112,96},{1... | collective-permute-start | bytes 196616 | tf_op jit(solution)/shard_map/ppermute | solution.py:368
  14.9 12.3 %collective-permute-start.1 = (bf16[128,512]{1,0:T(8,128)(2,1)S(1)}, bf16[128,512]{1,0:T(8,128)(2,1)S(1)}, u32[]{:S(2)}, u32[]{:S(2)}) collective-permute-start(bf16[128,512]{1,0:T(8,128)(2,1)S(1)} %maximum_select_fusion.near_ref), channel_id=1, source_target_pairs={{0,32},{16,48},{32,64},{48,80},{64,96},{80,112},{96,0},{112,16},{1... | collective-permute-start | bytes 393224 | tf_op jit(solution)/shard_map/ppermute | solution.py:376
  16.1 11.0 %collective-permute-start.2 = (bf16[128,512]{1,0:T(8,128)(2,1)S(1)}, bf16[128,512]{1,0:T(8,128)(2,1)S(1)}, u32[]{:S(2)}, u32[]{:S(2)}) collective-permute-start(bf16[128,512]{1,0:T(8,128)(2,1)S(1)} %maximum_select_fusion.near_ref), channel_id=1, source_target_pairs={{0,64},{16,80},{32,96},{48,112},{64,0},{80,16},{96,32},{112,48},{1... | collective-permute-start | bytes 393224 | tf_op jit(solution)/shard_map/ppermute | solution.py:376
  18.6 8.6 %collective-permute-start.3 = (bf16[128,512]{1,0:T(8,128)(2,1)S(1)}, bf16[128,512]{1,0:T(8,128)(2,1)S(1)}, u32[]{:S(2)}, u32[]{:S(2)}) collective-permute-start(bf16[128,512]{1,0:T(8,128)(2,1)S(1)} %maximum_select_fusion.near_ref), channel_id=1, source_target_pairs={{0,96},{16,112},{32,0},{48,16},{64,32},{80,48},{96,64},{112,80},{1... | collective-permute-start | bytes 393224 | tf_op jit(solution)/shard_map/ppermute | solution.py:376
  19.7 7.5 %copy-start.2 = (bf16[512,512]{1,0:T(8,128)(2,1)S(1)}, bf16[512,512]{1,0:T(8,128)(2,1)}, u32[]{:S(2)}) copy-start(bf16[512,512]{1,0:T(8,128)(2,1)} %w2_ref.3) | copy-start | bytes 1572868
  19.7 7.5 %copy-start.5 = (f32[512]{0:T(512)S(1)}, f32[512]{0:T(512)}, u32[]{:S(2)}) copy-start(f32[512]{0:T(512)} %param.28) | copy-start | bytes 6148
  27.3 40.2 %copy-start = (bf16[2,512,512]{2,1,0:T(8,128)(2,1)S(1)}, bf16[2,512,512]{2,1,0:T(8,128)(2,1)}, u32[]{:S(2)}) copy-start(bf16[2,512,512]{2,1,0:T(8,128)(2,1)} %w1_ref.5) | copy-start | bytes 3145732
  27.3 40.2 %copy-start.1 = (bf16[2,512,512]{2,1,0:T(8,128)(2,1)S(1)}, bf16[2,512,512]{2,1,0:T(8,128)(2,1)}, u32[]{:S(2)}) copy-start(bf16[2,512,512]{2,1,0:T(8,128)(2,1)} %w1_ref.4) | copy-start | bytes 3145732
  27.3 40.2 %copy-start.3 = (bf16[512,512]{1,0:T(8,128)(2,1)S(1)}, bf16[512,512]{1,0:T(8,128)(2,1)}, u32[]{:S(2)}) copy-start(bf16[512,512]{1,0:T(8,128)(2,1)} %w2_ref.4) | copy-start | bytes 1572868
  27.3 40.2 %copy-start.4 = (bf16[64,512]{1,0:T(8,128)(2,1)S(1)}, bf16[64,512]{1,0:T(8,128)(2,1)}, u32[]{:S(2)}) copy-start(bf16[64,512]{1,0:T(8,128)(2,1)} %nodes_ref.3) | copy-start | bytes 196612
  27.3 40.2 %copy-start.6 = (f32[512]{0:T(512)S(1)}, f32[512]{0:T(512)}, u32[]{:S(2)}) copy-start(f32[512]{0:T(512)} %param.31) | copy-start | bytes 6148
  27.3 40.2 %copy-start.7 = (s32[1,128,4]{1,2,0:T(4,128)S(1)}, s32[1,128,4]{1,2,0:T(4,128)}, u32[]{:S(2)}) copy-start(s32[1,128,4]{1,2,0:T(4,128)} %param.33) | copy-start | bytes 6148
  38.8 36.6 %copy-start.9 = (s32[1024,3]{0,1:T(4,128)S(1)}, s32[1024,3]{0,1:T(4,128)}, u32[]{:S(2)}) copy-start(s32[1024,3]{0,1:T(4,128)} %param.34) | copy-start | bytes 36868
  38.8 50.6 %copy-start.8 = (f32[512]{0:T(512)S(1)}, f32[512]{0:T(512)}, u32[]{:S(2)}) copy-start(f32[512]{0:T(512)} %param.37) | copy-start | bytes 6148
  69.7 19.7 %all-to-all-start.2 = ((bf16[128,16,128]{2,1,0:T(8,128)(2,1)}), bf16[128,16,128]{2,1,0:T(8,128)(2,1)S(1)}, u32[]{:S(2)}, u32[]{:S(2)}) async-start(bf16[128,16,128]{2,1,0:T(8,128)(2,1)} %get-tuple-element.22), calls=%async_computation.2 | async-start | bytes 1048576 | tf_op jit(solution)/shard_map/all_to_all | solution.py:462

commit v4 on v3

--- a/solution.py
+++ b/solution.py
@@ -187,20 +187,10 @@
         stream(edge_rows, out_ref, out_sems, k).wait()
 
 
-def grid_first_kernel(ids_ref, grid_ref, w1_ref, half_ref, hot_ref):
-    cells = grid_ref.shape[0]
+def grid_first_kernel(grid_ref, w1_ref, w2_ref, half_ref, centered_ref):
     half_ref[...] = (0.5 * dot(grid_ref[...], w1_ref[0])).astype(jnp.bfloat16)
-    per_peer = hot_ref.shape[1] // LANES
-    ids = ids_ref[...]
-    columns = jnp.transpose(lax.rem(ids, per_peer) * LANES + lax.div(ids, per_peer))
-    parts = CHUNK // LANES
-    fan = hot_ref.shape[0] // cells
-    for b in range(cells // CHUNK):
-        for e in range(fan):
-            start = (b * fan + e) * CHUNK
-            hot_ref[start : start + CHUNK, :] = stacked_hot(
-                columns, e * (cells // LANES) + b * parts, parts, hot_ref.shape[1]
-            )
+    w2 = w2_ref[...].astype(jnp.float32)
+    centered_ref[...] = (w2 - jnp.mean(w2, axis=-1, keepdims=True)).astype(jnp.bfloat16)
 
 
 def node_kernel(
@@ -226,7 +216,7 @@
 
 
 def decode_kernel(
-    hot_ref,
+    ids_ref,
     grid_ref,
     half_ref,
     received_ref,
@@ -235,75 +225,71 @@
     out_ref,
     received,
     w2,
-    hot,
     half,
     grid,
     wide,
     table,
     result,
     sems,
-    hot_sems,
-    half_sems,
     out_sems,
 ):
     cells = grid_ref.shape[0]
     blocks = cells // CHUNK
-    fan = hot_ref.shape[0] // cells
+    fan = ids_ref.shape[0] * LANES // cells
     peers, strips, _ = received_ref.shape
     groups = table.shape[1] // LANES
-
-    def stream(source, target, sems, k, rows):
-        place = pl.ds(k * rows, rows)
-        return pltpu.make_async_copy(source.at[place], target.at[place], sems.at[k])
-
-    received_copy = pltpu.make_async_copy(received_ref, received, sems.at[0])
-    w2_copy = pltpu.make_async_copy(w2_ref, w2, sems.at[1])
-    grid_copy = pltpu.make_async_copy(grid_ref, grid, sems.at[2])
-    def fetch(b):
-        stream(hot_ref, hot, hot_sems, b, fan * CHUNK).start()
-        stream(half_ref, half, half_sems, b, CHUNK).start()
-
-    received_copy.start()
-    fetch(0)
-    w2_copy.start()
-    received_copy.wait()
+    per_peer = strips // groups
+    pairs = ((received_ref, received), (half_ref, half), (w2_ref, w2), (grid_ref, grid))
+    copies = [
+        pltpu.make_async_copy(source, target, sems.at[k])
+        for k, (source, target) in enumerate(pairs)
+    ]
+    for copy in copies:
+        copy.start()
+
+    span = cells // out_sems.shape[0]
+    outs = [
+        pltpu.make_async_copy(
+            result.at[pl.ds(k * span, span)], out_ref.at[pl.ds(k * span, span)], out_sems.at[k]
+        )
+        for k in range(out_sems.shape[0])
+    ]
+    copies[0].wait()
     wide[...] = received[...].astype(jnp.float32).reshape(wide.shape)
-    for j in range(strips // groups):
+    for j in range(per_peer):
         for q in range(groups):
             table[j * peers : (j + 1) * peers, q * LANES : (q + 1) * LANES] = wide[
                 pl.ds(j * groups + q, peers, stride=strips), :
             ].astype(jnp.bfloat16)
+    ids = ids_ref[...]
+    columns = jnp.transpose(lax.rem(ids, per_peer) * peers + lax.div(ids, per_peer))
+    for copy in copies[1:]:
+        copy.wait()
 
     def first(b, e):
-        if e == 0:
-            stream(hot_ref, hot, hot_sems, b, fan * CHUNK).wait()
-            stream(half_ref, half, half_sems, b, CHUNK).wait()
-            if b == 0:
-                grid_copy.start()
-            if b + 1 < blocks:
-                fetch(b + 1)
-        rows = pl.ds((b * fan + e) * CHUNK, CHUNK)
+        parts = CHUNK // LANES
+        hot = stacked_hot(columns, e * (cells // LANES) + b * parts, parts, table.shape[0])
         known = half[b * CHUNK : (b + 1) * CHUNK, :].astype(jnp.float32)
-        return silu_half(known + dot(hot[rows, :], table[...]))
+        return silu_half(known + dot(hot, table[...]))
 
     work = [(b, e) for b in range(blocks) for e in range(fan)]
     hidden = first(*work[0])
-    w2_copy.wait()
     for k, (b, e) in enumerate(work):
         later = first(*work[k + 1]) if k + 1 < len(work) else None
-        center, scale = center_scale(dot(hidden, w2[...]))
-        message = center * scale if e == 0 else message + center * scale
+        center = dot(hidden, w2[...])
+        spread = jnp.mean(center * center, axis=-1, keepdims=True)
+        scaled = center * lax.rsqrt(spread + EPSILON)
+        message = scaled if e == 0 else message + scaled
         hidden = later
         if e == fan - 1:
-            if b == 0:
-                grid_copy.wait()
-            part = pl.ds(b * CHUNK, CHUNK)
+            part = slice(b * CHUNK, (b + 1) * CHUNK)
             result[part, :] = (
                 grid[part, :].astype(jnp.float32) + message * gain_ref[...]
             ).astype(jnp.bfloat16)
-            stream(result, out_ref, out_sems, b, CHUNK).start()
-    for b in range(blocks):
-        stream(result, out_ref, out_sems, b, CHUNK).wait()
+            if (b + 1) * CHUNK % span == 0:
+                outs[(b + 1) * CHUNK // span - 1].start()
+    for out in outs:
+        out.wait()
 
 
 def whole(array):
@@ -461,47 +447,43 @@
 
     received = lax.all_to_all(picked, ("row", "col"), 0, 0, tiled=True)
     dec_scale = dec_gain.reshape(1, width)
-    dec_blocks = cells // CHUNK
-    grid_half, dec_hot = pl.pallas_call(
+    grid_half, dec_centered = pl.pallas_call(
         grid_first_kernel,
         grid=(1,),
-        in_specs=[pl.BlockSpec((fan * cells // LANES, LANES), lambda i: (0, 0)), whole(grid), layer(0, width)],
+        in_specs=[whole(grid), layer(0, width), whole(dec_w2)],
         out_specs=(
             pl.BlockSpec((cells, width), lambda i: (0, 0)),
-            pl.BlockSpec((fan * cells, peers * per_peer), lambda i: (0, 0)),
+            pl.BlockSpec((width, width), lambda i: (0, 0)),
         ),
         out_shape=(
             jax.ShapeDtypeStruct((cells, width), bf16),
-            jax.ShapeDtypeStruct((fan * cells, peers * per_peer), bf16),
+            jax.ShapeDtypeStruct((width, width), bf16),
         ),
         compiler_params=params(57),
         cost_estimate=pl.CostEstimate(
             flops=2 * cells * width * width, bytes_accessed=6 * cells * width, transcendentals=0
         ),
         name="grid_first",
-    )(dec_index.T.reshape(-1, LANES), grid, dec_w1)
+    )(grid, dec_w1, dec_w2)
     grid_out = pl.pallas_call(
         decode_kernel,
-        in_specs=[hbm] * 5 + [vmem],
+        in_specs=[vmem] + [hbm] * 4 + [vmem],
         out_specs=hbm,
         out_shape=jax.ShapeDtypeStruct((cells, width), bf16),
         scratch_shapes=[
             pltpu.VMEM(received.shape, bf16),
             pltpu.VMEM(dec_w2.shape, bf16),
-            pltpu.VMEM(dec_hot.shape, bf16),
             pltpu.VMEM(grid_half.shape, bf16),
             pltpu.VMEM(grid.shape, bf16),
             pltpu.VMEM((peers * strips, LANES), f32),
             pltpu.VMEM((peers * per_peer, width), bf16),
             pltpu.VMEM((cells, width), bf16),
-            pltpu.SemaphoreType.DMA((3,)),
-            pltpu.SemaphoreType.DMA((dec_blocks,)),
-            pltpu.SemaphoreType.DMA((dec_blocks,)),
-            pltpu.SemaphoreType.DMA((dec_blocks,)),
+            pltpu.SemaphoreType.DMA((4,)),
+            pltpu.SemaphoreType.DMA((2,)),
         ],
         compiler_params=params(53),
         name="decoder",
-    )(dec_hot, grid, grid_half, received, dec_w2, dec_scale)
+    )(dec_index.T.reshape(-1, LANES), grid, grid_half, received, dec_centered, dec_scale)
     return (nodes_out, edges_out.reshape(edges.shape), grid_out)
 
 

time: 97.6 us -> 96.1 us (0.985)
  Pallas kernels: 35.3 us -> 29.9 us
  blocking collectives: 28.7 us -> 33.2 us
  waiting for transfers between devices: 9.66 us -> 11 us
    all_to_all x1, blocking collectives: 28.7 us -> 33.2 us  [on_device(): lax.all_to_all(partial_sum.reshape(col_size, block, width), 'col', 0, 0,...]
    pallas_call x1, Pallas kernels: 11.5 us -> 7.94 us  [on_device(): pl.pallas_call(edge_kernel, in_specs=[smem, vmem, hbm, hbm] + [vmem] * (4...]
    pallas_call x2, Pallas kernels: 11.8 us -> 9.89 us  [the longest x1 6.48 us: on_device(): pl.pallas_call(decode_kernel, in_specs=[vmem] + [hbm] * 4 + [vmem], out_s...]
    all_to_all x1, waiting for transfers between devices: 9.23 us -> 10.6 us  [on_device(): received = lax.all_to_all(picked, ('row', 'col'), 0, 0, tiled=True)]
  transfers between devices with their start and end apart: 6 -> 6, of which waited for: 3 -> 3; matrix products, arithmetic and copies ran while one was open for 2% -> 1% of each run, Pallas kernels for 12% -> 11%
where the time goes in v4:
time: 96.1 us
  blocking collectives  33.2 us (35%)
  Pallas kernels  29.9 us (31%)
  starting transfers between devices  19.3 us (20%)
  waiting for transfers between devices  11 us (11%)
  between operations  1.64 us (2%)
  other arithmetic  1.03 us (1%)
    all_to_all x1, blocking collectives, on_device(): lax.all_to_all(partial_sum.reshape(col_size, block, width), 'col', 0, 0,...  33.2 us
    all_to_all x1, waiting for transfers between devices, on_device(): received = lax.all_to_all(picked, ('row', 'col'), 0, 0, tiled=True)  10.6 us
    all_to_all x1, starting transfers between devices, on_device(): lax.all_to_all(recv_copies, 'col', 0, 0, tiled=True).reshape(-1, width)  8.6 us
    pallas_call x1, Pallas kernels, on_device(): pl.pallas_call(edge_kernel, in_specs=[smem, vmem, hbm, hbm] + [vmem] * (4...  7.94 us
    pallas_call x1, Pallas kernels, on_device(): pl.pallas_call(edge_first_kernel, in_specs=[vmem, hbm, hbm, vmem], out_sp...  7.41 us
    pallas_call x1, Pallas kernels, on_device(): pl.pallas_call(decode_kernel, in_specs=[vmem] + [hbm] * 4 + [vmem], out_s...  6.48 us
    ppermute x3, starting transfers between devices, on_device(): lax.ppermute(near, 'row', [(i, (i + 2 * k) % row_size) for i in range(row...  4.88 us
    all_to_all x1, starting transfers between devices, on_device(): received = lax.all_to_all(picked, ('row', 'col'), 0, 0, tiled=True)  4.78 us
  transfers between devices with their start and end apart: 6, of which 3 were waited for; matrix products, arithmetic and copies ran while one was open for 1% of the time, Pallas kernels for 11%

profile of v4, /device:TPU:1, one launch (start us, length us, event | category | flops | bytes accessed | tf_op | source)
XLA Modules:
  0.0 96.1 jit_solution(5285483261478224701)
XLA Ops:
  0.7 2.5 %project.1 = (bf16[64,512]{1,0:T(8,128)(2,1)}, bf16[16,64,512]{2,1,0:T(8,128)(2,1)}) custom-call(bf16[64,512]{1,0:T(8,128)(2,1)} %nodes_ref.3, bf16[3,512,512]{2,1,0:T(8,128)(2,1)} %w1_ref.3, bf16[3,512,512]{2,1,0:T(8,128)(2,1)} %w1_ref.3), custom_call_target="tpu_custom_call" | custom-call | tf_op jit(solution)/shard_map/project/pallas_call | solution.py:337
  3.2 8.6 %all-to-all-start = ((bf16[16,64,512]{2,1,0:T(8,128)(2,1)}), bf16[16,64,512]{2,1,0:T(8,128)(2,1)S(1)}, u32[]{:S(2)}, u32[]{:S(2)}) async-start(bf16[16,64,512]{2,1,0:T(8,128)(2,1)} %get-tuple-element.16), calls=%async_computation | async-start | bytes 2097152 | tf_op jit(solution)/shard_map/all_to_all | solution.py:352
  11.8 1.0 %collective-permute-start = (bf16[64,512]{1,0:T(8,128)(2,1)}, bf16[64,512]{1,0:T(8,128)(2,1)S(1)}, u32[]{:S(2)}, u32[]{:S(2)}) collective-permute-start(bf16[64,512]{1,0:T(8,128)(2,1)} %get-tuple-element.13), channel_id=1, source_target_pairs={{0,16},{16,0},{32,48},{48,32},{64,80},{80,64},{96,112},{112,96},{1... | collective-permute-start | bytes 196616 | tf_op jit(solution)/shard_map/ppermute | solution.py:354
  13.5 0.1 pad_add_fusion.1.place_ref
  13.6 0.3 collective-permute-done
  13.9 0.9 maximum_select_fusion.near_ref
  14.9 1.3 %collective-permute-start.1 = (bf16[128,512]{1,0:T(8,128)(2,1)S(1)}, bf16[128,512]{1,0:T(8,128)(2,1)S(1)}, u32[]{:S(2)}, u32[]{:S(2)}) collective-permute-start(bf16[128,512]{1,0:T(8,128)(2,1)S(1)} %maximum_select_fusion.near_ref), channel_id=1, source_target_pairs={{0,32},{16,48},{32,64},{48,80},{64,96},{80,112},{96,0},{112,16},{1... | collective-permute-start | bytes 393224 | tf_op jit(solution)/shard_map/ppermute | solution.py:362
  16.1 2.4 %collective-permute-start.2 = (bf16[128,512]{1,0:T(8,128)(2,1)S(1)}, bf16[128,512]{1,0:T(8,128)(2,1)S(1)}, u32[]{:S(2)}, u32[]{:S(2)}) collective-permute-start(bf16[128,512]{1,0:T(8,128)(2,1)S(1)} %maximum_select_fusion.near_ref), channel_id=1, source_target_pairs={{0,64},{16,80},{32,96},{48,112},{64,0},{80,16},{96,32},{112,48},{1... | collective-permute-start | bytes 393224 | tf_op jit(solution)/shard_map/ppermute | solution.py:362
  18.6 1.2 %collective-permute-start.3 = (bf16[128,512]{1,0:T(8,128)(2,1)S(1)}, bf16[128,512]{1,0:T(8,128)(2,1)S(1)}, u32[]{:S(2)}, u32[]{:S(2)}) collective-permute-start(bf16[128,512]{1,0:T(8,128)(2,1)S(1)} %maximum_select_fusion.near_ref), channel_id=1, source_target_pairs={{0,96},{16,112},{32,0},{48,16},{64,32},{80,48},{96,64},{112,80},{1... | collective-permute-start | bytes 393224 | tf_op jit(solution)/shard_map/ppermute | solution.py:362
  19.7 7.4 %edge_first.1.half_ref = bf16[4096,512]{1,0:T(8,128)(2,1)} custom-call(s32[4,8,128]{2,1,0:T(8,128)} %bitcast.25, bf16[4096,512]{1,0:T(8,128)(2,1)} %bitcast.23, bf16[3,512,512]{2,1,0:T(8,128)(2,1)} %w1_ref.3, bf16[7,512]{1,0:T(8,128)(2,1)} %bias_ref.1), custom_call_target="tpu_custom_call" | custom-call | flops 2147483648 | bytes 4194304 | tf_op jit(solution)/shard_map/edge_first/pallas_call | solution.py:369
  27.2 0.0 collective-permute-done.2.far2_ref
  27.2 0.1 all-to-all-done
  27.3 0.0 copy-start.3
  27.3 0.0 copy-start.4
  27.3 0.0 copy-start.6
  27.3 0.0 copy-start.7
  27.3 7.9 %edges.1 = (bf16[4096,512]{1,0:T(8,128)(2,1)}, bf16[1024,512]{1,0:T(8,128)(2,1)S(1)}) custom-call(s32[2]{0:T(128)S(1)} %pad_add_fusion.1.place_ref, s32[4,16,128]{2,1,0:T(8,128)S(1)} %pad_add_fusion.ids_ref, bf16[4096,512]{1,0:T(8,128)(2,1)} %bitcast.24, bf16[4096,512]{1,0:T(8,128)(2,1)} %edge_first.1.half_ref, ...), custom_call_target="tpu_custom_call" | custom-call | tf_op jit(solution)/shard_map/edges/pallas_call | solution.py:395
  35.3 0.0 copy-start.9
  35.3 33.2 %all_to_all.15.parts_ref = bf16[16,64,512]{2,1,0:T(8,128)(2,1)S(1)} all-to-all(bf16[16,64,512]{2,1,0:T(8,128)(2,1)S(1)} %bitcast.18), channel_id=1, replica_groups=mesh['row'=8,'col'=16] {'col'}, dimensions={0} | all-to-all | bytes 2097152 | tf_op jit(solution)/shard_map/all_to_all | solution.py:417
  68.5 2.1 %nodes.1 = (bf16[64,512]{1,0:T(8,128)(2,1)}, bf16[128,16,128]{2,1,0:T(8,128)(2,1)}) custom-call(bf16[16,64,512]{2,1,0:T(8,128)(2,1)S(1)} %all_to_all.15.parts_ref, bf16[64,512]{1,0:T(8,128)(2,1)S(1)} %copy-done.4, bf16[2,512,512]{2,1,0:T(8,128)(2,1)S(1)} %copy-done.1, bf16[512,512]{1,0:T(8,128)(2,1)S(1)} %copy-done.3, f32[1,512]{1,0:T(1,128)S(1)} %bitcast.20, ...), custom_call_target="tpu_custom_call" | custom-call | tf_op jit(solution)/shard_map/nodes/pallas_call | solution.py:423
  70.6 4.8 %all-to-all-start.2 = ((bf16[128,16,128]{2,1,0:T(8,128)(2,1)}), bf16[128,16,128]{2,1,0:T(8,128)(2,1)S(1)}, u32[]{:S(2)}, u32[]{:S(2)}) async-start(bf16[128,16,128]{2,1,0:T(8,128)(2,1)} %get-tuple-element.21), calls=%async_computation.2 | async-start | bytes 1048576 | tf_op jit(solution)/shard_map/all_to_all | solution.py:448
  75.5 3.4 %grid_first.1 = (bf16[1024,512]{1,0:T(8,128)(2,1)}, bf16[512,512]{1,0:T(8,128)(2,1)}) custom-call(bf16[1024,512]{1,0:T(8,128)(2,1)} %grid_ref.3, bf16[2,512,512]{2,1,0:T(8,128)(2,1)} %w1_ref.5, bf16[512,512]{1,0:T(8,128)(2,1)} %w2_ref.5), custom_call_target="tpu_custom_call" | custom-call | flops 536870912 | bytes 3145728 | tf_op jit(solution)/shard_map/grid_first/pallas_call | solution.py:450
  78.9 10.6 %all-to-all-done.2.received_ref = bf16[128,16,128]{2,1,0:T(8,128)(2,1)S(1)} async-done(((bf16[128,16,128]{2,1,0:T(8,128)(2,1)}), bf16[128,16,128]{2,1,0:T(8,128)(2,1)S(1)}, u32[]{:S(2)}, u32[]{:S(2)}) %all-to-all-start.2) | async-done | bytes 524320 | tf_op jit(solution)/shard_map/all_to_all | solution.py:448
  89.4 6.5 %decoder.1 = bf16[1024,512]{1,0:T(8,128)(2,1)} custom-call(s32[24,128]{1,0:T(8,128)S(1)} %reshape.48.ids_ref, bf16[1024,512]{1,0:T(8,128)(2,1)} %grid_ref.3, bf16[1024,512]{1,0:T(8,128)(2,1)} %get-tuple-element.20.half_ref, bf16[128,16,128]{2,1,0:T(8,128)(2,1)S(1)} %all-to-all-done.2.received_ref, bf16[512,512]{1,0:T(8,128)(2,1)} %get-tuple-element.22.w2_ref, ...), custom_call_target="tpu_custom_call" | custom-call | tf_op jit(solution)/shard_map/decoder/pallas_call | solution.py:468
  (23 shorter events, 0.1 us)
Async XLA Ops:
  0.6 12.8 %copy-start.11 = (s32[1,1,4096]{2,1,0:T(1,128)S(1)}, s32[1,1,4096]{2,1,0:T(1,128)}, u32[]{:S(2)}) copy-start(s32[1,1,4096]{2,1,0:T(1,128)} %param.21) | copy-start | bytes 49156
  0.6 12.8 %copy-start.10 = (s32[1,1,4096]{2,1,0:T(1,128)S(1)}, s32[1,1,4096]{2,1,0:T(1,128)}, u32[]{:S(2)}) copy-start(s32[1,1,4096]{2,1,0:T(1,128)} %param.22) | copy-start | bytes 49156
  3.2 24.1 %all-to-all-start = ((bf16[16,64,512]{2,1,0:T(8,128)(2,1)}), bf16[16,64,512]{2,1,0:T(8,128)(2,1)S(1)}, u32[]{:S(2)}, u32[]{:S(2)}) async-start(bf16[16,64,512]{2,1,0:T(8,128)(2,1)} %get-tuple-element.16), calls=%async_computation | async-start | bytes 2097152 | tf_op jit(solution)/shard_map/all_to_all | solution.py:352
  11.8 2.1 %collective-permute-start = (bf16[64,512]{1,0:T(8,128)(2,1)}, bf16[64,512]{1,0:T(8,128)(2,1)S(1)}, u32[]{:S(2)}, u32[]{:S(2)}) collective-permute-start(bf16[64,512]{1,0:T(8,128)(2,1)} %get-tuple-element.13), channel_id=1, source_target_pairs={{0,16},{16,0},{32,48},{48,32},{64,80},{80,64},{96,112},{112,96},{1... | collective-permute-start | bytes 196616 | tf_op jit(solution)/shard_map/ppermute | solution.py:354
  14.9 12.3 %collective-permute-start.1 = (bf16[128,512]{1,0:T(8,128)(2,1)S(1)}, bf16[128,512]{1,0:T(8,128)(2,1)S(1)}, u32[]{:S(2)}, u32[]{:S(2)}) collective-permute-start(bf16[128,512]{1,0:T(8,128)(2,1)S(1)} %maximum_select_fusion.near_ref), channel_id=1, source_target_pairs={{0,32},{16,48},{32,64},{48,80},{64,96},{80,112},{96,0},{112,16},{1... | collective-permute-start | bytes 393224 | tf_op jit(solution)/shard_map/ppermute | solution.py:362
  16.1 11.0 %collective-permute-start.2 = (bf16[128,512]{1,0:T(8,128)(2,1)S(1)}, bf16[128,512]{1,0:T(8,128)(2,1)S(1)}, u32[]{:S(2)}, u32[]{:S(2)}) collective-permute-start(bf16[128,512]{1,0:T(8,128)(2,1)S(1)} %maximum_select_fusion.near_ref), channel_id=1, source_target_pairs={{0,64},{16,80},{32,96},{48,112},{64,0},{80,16},{96,32},{112,48},{1... | collective-permute-start | bytes 393224 | tf_op jit(solution)/shard_map/ppermute | solution.py:362
  18.6 8.6 %collective-permute-start.3 = (bf16[128,512]{1,0:T(8,128)(2,1)S(1)}, bf16[128,512]{1,0:T(8,128)(2,1)S(1)}, u32[]{:S(2)}, u32[]{:S(2)}) collective-permute-start(bf16[128,512]{1,0:T(8,128)(2,1)S(1)} %maximum_select_fusion.near_ref), channel_id=1, source_target_pairs={{0,96},{16,112},{32,0},{48,16},{64,32},{80,48},{96,64},{112,80},{1... | collective-permute-start | bytes 393224 | tf_op jit(solution)/shard_map/ppermute | solution.py:362
  19.7 7.5 %copy-start.2 = (bf16[512,512]{1,0:T(8,128)(2,1)S(1)}, bf16[512,512]{1,0:T(8,128)(2,1)}, u32[]{:S(2)}) copy-start(bf16[512,512]{1,0:T(8,128)(2,1)} %w2_ref.3) | copy-start | bytes 1572868
  19.7 7.5 %copy-start.5 = (f32[512]{0:T(512)S(1)}, f32[512]{0:T(512)}, u32[]{:S(2)}) copy-start(f32[512]{0:T(512)} %param.28) | copy-start | bytes 6148
  27.3 41.2 %copy-start = (bf16[2,512,512]{2,1,0:T(8,128)(2,1)S(1)}, bf16[2,512,512]{2,1,0:T(8,128)(2,1)}, u32[]{:S(2)}) copy-start(bf16[2,512,512]{2,1,0:T(8,128)(2,1)} %w1_ref.5) | copy-start | bytes 3145732
  27.3 41.2 %copy-start.1 = (bf16[2,512,512]{2,1,0:T(8,128)(2,1)S(1)}, bf16[2,512,512]{2,1,0:T(8,128)(2,1)}, u32[]{:S(2)}) copy-start(bf16[2,512,512]{2,1,0:T(8,128)(2,1)} %w1_ref.4) | copy-start | bytes 3145732
  27.3 41.2 %copy-start.3 = (bf16[512,512]{1,0:T(8,128)(2,1)S(1)}, bf16[512,512]{1,0:T(8,128)(2,1)}, u32[]{:S(2)}) copy-start(bf16[512,512]{1,0:T(8,128)(2,1)} %w2_ref.4) | copy-start | bytes 1572868
  27.3 41.2 %copy-start.4 = (bf16[64,512]{1,0:T(8,128)(2,1)S(1)}, bf16[64,512]{1,0:T(8,128)(2,1)}, u32[]{:S(2)}) copy-start(bf16[64,512]{1,0:T(8,128)(2,1)} %nodes_ref.3) | copy-start | bytes 196612
  27.3 41.2 %copy-start.6 = (f32[512]{0:T(512)S(1)}, f32[512]{0:T(512)}, u32[]{:S(2)}) copy-start(f32[512]{0:T(512)} %param.31) | copy-start | bytes 6148
  27.3 41.2 %copy-start.7 = (s32[1,128,4]{1,2,0:T(4,128)S(1)}, s32[1,128,4]{1,2,0:T(4,128)}, u32[]{:S(2)}) copy-start(s32[1,128,4]{1,2,0:T(4,128)} %param.33) | copy-start | bytes 6148
  35.3 40.1 %copy-start.9 = (s32[1024,3]{0,1:T(4,128)S(1)}, s32[1024,3]{0,1:T(4,128)}, u32[]{:S(2)}) copy-start(s32[1024,3]{0,1:T(4,128)} %param.34) | copy-start | bytes 36868
  68.5 21.0 %copy-start.8 = (f32[512]{0:T(512)S(1)}, f32[512]{0:T(512)}, u32[]{:S(2)}) copy-start(f32[512]{0:T(512)} %param.37) | copy-start | bytes 6148
  70.6 18.8 %all-to-all-start.2 = ((bf16[128,16,128]{2,1,0:T(8,128)(2,1)}), bf16[128,16,128]{2,1,0:T(8,128)(2,1)S(1)}, u32[]{:S(2)}, u32[]{:S(2)}) async-start(bf16[128,16,128]{2,1,0:T(8,128)(2,1)} %get-tuple-element.21), calls=%async_computation.2 | async-start | bytes 1048576 | tf_op jit(solution)/shard_map/all_to_all | solution.py:448

commit v5 on v4

--- a/solution.py
+++ b/solution.py
@@ -27,8 +27,22 @@
 
 
 def column_hot(ids, count):
-    lanes = lax.broadcasted_iota(jnp.int32, (ids.shape[0], count), 1)
-    return (ids == lanes).astype(jnp.bfloat16)
+    one, zero = jnp.ones((), jnp.bfloat16), jnp.zeros((), jnp.bfloat16)
+    if count % LANES:
+        lanes = lax.broadcasted_iota(jnp.int32, (ids.shape[0], count), 1)
+        return (ids == lanes).astype(jnp.bfloat16)
+    shape = (ids.shape[0], LANES)
+    lane = lax.broadcasted_iota(jnp.int32, shape, 1).astype(jnp.float32).astype(jnp.bfloat16)
+    low = jnp.broadcast_to((ids & (LANES - 1)).astype(jnp.float32).astype(jnp.bfloat16), shape)
+    high = jnp.broadcast_to(lax.div(ids, LANES).astype(jnp.float32).astype(jnp.bfloat16), shape)
+    hit = jnp.where(low == lane, one, zero)
+    return jnp.concatenate(
+        [
+            jnp.where(high == jnp.asarray(strip, jnp.bfloat16), hit, zero)
+            for strip in range(count // LANES)
+        ],
+        axis=1,
+    )
 
 
 def stacked_hot(columns, first, number, count):
@@ -38,8 +52,9 @@
 
 
 def row_hot(ids, count):
-    rows = lax.broadcasted_iota(jnp.int32, (count, ids.shape[1]), 0)
-    return (ids == rows).astype(jnp.bfloat16)
+    rows = lax.broadcasted_iota(jnp.int16, (count, ids.shape[1]), 0)
+    one, zero = jnp.ones((), jnp.bfloat16), jnp.zeros((), jnp.bfloat16)
+    return jnp.where(ids.astype(jnp.int16) == rows, one, zero)
 
 
 def project_kernel(nodes_ref, send_weight_ref, recv_weight_ref, send_ref, recv_ref):

time: 96.1 us -> 95.2 us (level)
  blocking collectives: 33.2 us -> 25.2 us
  Pallas kernels: 29.9 us -> 36.4 us
  starting transfers between devices: 19.3 us -> 20.3 us
    all_to_all x1, blocking collectives: 33.2 us -> 25.2 us  [on_device(): lax.all_to_all(partial_sum.reshape(col_size, block, width), 'col', 0, 0,...]
    pallas_call x1, Pallas kernels: 7.94 us -> 14.4 us  [on_device(): pl.pallas_call(edge_kernel, in_specs=[smem, vmem, hbm, hbm] + [vmem] * (4...]
    all_to_all x1, starting transfers between devices: 4.78 us -> 5.77 us  [on_device(): received = lax.all_to_all(picked, ('row', 'col'), 0, 0, tiled=True)]
where the time goes in v5:
time: 95.2 us; the launch traced here: 95.6 us
  Pallas kernels  36.4 us (38%)
  blocking collectives  25.2 us (26%)
  starting transfers between devices  20.3 us (21%)
  waiting for transfers between devices  11 us (12%)
  between operations  1.64 us (2%)
  other arithmetic  1.03 us (1%)
    all_to_all x1, blocking collectives, on_device(): lax.all_to_all(partial_sum.reshape(col_size, block, width), 'col', 0, 0,...  25.2 us
    pallas_call x1, Pallas kernels, on_device(): pl.pallas_call(edge_kernel, in_specs=[smem, vmem, hbm, hbm] + [vmem] * (4...  14.4 us
    all_to_all x1, waiting for transfers between devices, on_device(): received = lax.all_to_all(picked, ('row', 'col'), 0, 0, tiled=True)  10.6 us
    all_to_all x1, starting transfers between devices, on_device(): lax.all_to_all(recv_copies, 'col', 0, 0, tiled=True).reshape(-1, width)  8.6 us
    pallas_call x1, Pallas kernels, on_device(): pl.pallas_call(edge_first_kernel, in_specs=[vmem, hbm, hbm, vmem], out_sp...  7.41 us
    pallas_call x1, Pallas kernels, on_device(): pl.pallas_call(decode_kernel, in_specs=[vmem] + [hbm] * 4 + [vmem], out_s...  6.5 us
    all_to_all x1, starting transfers between devices, on_device(): received = lax.all_to_all(picked, ('row', 'col'), 0, 0, tiled=True)  5.77 us
    ppermute x3, starting transfers between devices, on_device(): lax.ppermute(near, 'row', [(i, (i + 2 * k) % row_size) for i in range(row...  4.88 us
  transfers between devices with their start and end apart: 6, of which 3 were waited for; matrix products, arithmetic and copies ran while one was open for 1% of the time, Pallas kernels for 11%

profile of v5, /device:TPU:1, one launch (start us, length us, event | category | flops | bytes accessed | tf_op | source)
XLA Modules:
  0.0 95.6 jit_solution(10765132010436436650)
XLA Ops:
  0.7 2.5 %project.1 = (bf16[64,512]{1,0:T(8,128)(2,1)}, bf16[16,64,512]{2,1,0:T(8,128)(2,1)}) custom-call(bf16[64,512]{1,0:T(8,128)(2,1)} %nodes_ref.3, bf16[3,512,512]{2,1,0:T(8,128)(2,1)} %w1_ref.3, bf16[3,512,512]{2,1,0:T(8,128)(2,1)} %w1_ref.3), custom_call_target="tpu_custom_call" | custom-call | tf_op jit(solution)/shard_map/project/pallas_call | solution.py:352
  3.2 8.6 %all-to-all-start = ((bf16[16,64,512]{2,1,0:T(8,128)(2,1)}), bf16[16,64,512]{2,1,0:T(8,128)(2,1)S(1)}, u32[]{:S(2)}, u32[]{:S(2)}) async-start(bf16[16,64,512]{2,1,0:T(8,128)(2,1)} %get-tuple-element.16), calls=%async_computation | async-start | bytes 2097152 | tf_op jit(solution)/shard_map/all_to_all | solution.py:367
  11.8 1.0 %collective-permute-start = (bf16[64,512]{1,0:T(8,128)(2,1)}, bf16[64,512]{1,0:T(8,128)(2,1)S(1)}, u32[]{:S(2)}, u32[]{:S(2)}) collective-permute-start(bf16[64,512]{1,0:T(8,128)(2,1)} %get-tuple-element.13), channel_id=1, source_target_pairs={{0,16},{16,0},{32,48},{48,32},{64,80},{80,64},{96,112},{112,96},{1... | collective-permute-start | bytes 196616 | tf_op jit(solution)/shard_map/ppermute | solution.py:369
  13.5 0.1 pad_add_fusion.1.place_ref
  13.6 0.3 collective-permute-done
  13.9 0.9 maximum_select_fusion.near_ref
  14.9 1.3 %collective-permute-start.1 = (bf16[128,512]{1,0:T(8,128)(2,1)S(1)}, bf16[128,512]{1,0:T(8,128)(2,1)S(1)}, u32[]{:S(2)}, u32[]{:S(2)}) collective-permute-start(bf16[128,512]{1,0:T(8,128)(2,1)S(1)} %maximum_select_fusion.near_ref), channel_id=1, source_target_pairs={{0,32},{16,48},{32,64},{48,80},{64,96},{80,112},{96,0},{112,16},{1... | collective-permute-start | bytes 393224 | tf_op jit(solution)/shard_map/ppermute | solution.py:377
  16.1 2.4 %collective-permute-start.2 = (bf16[128,512]{1,0:T(8,128)(2,1)S(1)}, bf16[128,512]{1,0:T(8,128)(2,1)S(1)}, u32[]{:S(2)}, u32[]{:S(2)}) collective-permute-start(bf16[128,512]{1,0:T(8,128)(2,1)S(1)} %maximum_select_fusion.near_ref), channel_id=1, source_target_pairs={{0,64},{16,80},{32,96},{48,112},{64,0},{80,16},{96,32},{112,48},{1... | collective-permute-start | bytes 393224 | tf_op jit(solution)/shard_map/ppermute | solution.py:377
  18.6 1.2 %collective-permute-start.3 = (bf16[128,512]{1,0:T(8,128)(2,1)S(1)}, bf16[128,512]{1,0:T(8,128)(2,1)S(1)}, u32[]{:S(2)}, u32[]{:S(2)}) collective-permute-start(bf16[128,512]{1,0:T(8,128)(2,1)S(1)} %maximum_select_fusion.near_ref), channel_id=1, source_target_pairs={{0,96},{16,112},{32,0},{48,16},{64,32},{80,48},{96,64},{112,80},{1... | collective-permute-start | bytes 393224 | tf_op jit(solution)/shard_map/ppermute | solution.py:377
  19.7 7.4 %edge_first.1.half_ref = bf16[4096,512]{1,0:T(8,128)(2,1)} custom-call(s32[4,8,128]{2,1,0:T(8,128)} %bitcast.25, bf16[4096,512]{1,0:T(8,128)(2,1)} %bitcast.23, bf16[3,512,512]{2,1,0:T(8,128)(2,1)} %w1_ref.3, bf16[7,512]{1,0:T(8,128)(2,1)} %bias_ref.1), custom_call_target="tpu_custom_call" | custom-call | flops 2147483648 | bytes 4194304 | tf_op jit(solution)/shard_map/edge_first/pallas_call | solution.py:384
  27.2 0.0 collective-permute-done.2.far2_ref
  27.2 0.1 all-to-all-done
  27.3 0.0 copy-start.3
  27.3 0.0 copy-start.4
  27.3 0.0 copy-start.6
  27.3 0.0 copy-start.7
  27.3 14.4 %edges.1 = (bf16[4096,512]{1,0:T(8,128)(2,1)}, bf16[1024,512]{1,0:T(8,128)(2,1)S(1)}) custom-call(s32[2]{0:T(128)S(1)} %pad_add_fusion.1.place_ref, s32[4,16,128]{2,1,0:T(8,128)S(1)} %pad_add_fusion.ids_ref, bf16[4096,512]{1,0:T(8,128)(2,1)} %bitcast.24, bf16[4096,512]{1,0:T(8,128)(2,1)} %edge_first.1.half_ref, ...), custom_call_target="tpu_custom_call" | custom-call | tf_op jit(solution)/shard_map/edges/pallas_call | solution.py:410
  41.7 0.0 copy-start.9
  41.8 25.2 %all_to_all.15.parts_ref = bf16[16,64,512]{2,1,0:T(8,128)(2,1)S(1)} all-to-all(bf16[16,64,512]{2,1,0:T(8,128)(2,1)S(1)} %bitcast.18), channel_id=1, replica_groups=mesh['row'=8,'col'=16] {'col'}, dimensions={0} | all-to-all | bytes 2097152 | tf_op jit(solution)/shard_map/all_to_all | solution.py:432
  67.0 2.1 %nodes.1 = (bf16[64,512]{1,0:T(8,128)(2,1)}, bf16[128,16,128]{2,1,0:T(8,128)(2,1)}) custom-call(bf16[16,64,512]{2,1,0:T(8,128)(2,1)S(1)} %all_to_all.15.parts_ref, bf16[64,512]{1,0:T(8,128)(2,1)S(1)} %copy-done.4, bf16[2,512,512]{2,1,0:T(8,128)(2,1)S(1)} %copy-done.1, bf16[512,512]{1,0:T(8,128)(2,1)S(1)} %copy-done.3, f32[1,512]{1,0:T(1,128)S(1)} %bitcast.20, ...), custom_call_target="tpu_custom_call" | custom-call | tf_op jit(solution)/shard_map/nodes/pallas_call | solution.py:438
  69.2 5.8 %all-to-all-start.2 = ((bf16[128,16,128]{2,1,0:T(8,128)(2,1)}), bf16[128,16,128]{2,1,0:T(8,128)(2,1)S(1)}, u32[]{:S(2)}, u32[]{:S(2)}) async-start(bf16[128,16,128]{2,1,0:T(8,128)(2,1)} %get-tuple-element.21), calls=%async_computation.2 | async-start | bytes 1048576 | tf_op jit(solution)/shard_map/all_to_all | solution.py:463
  75.0 3.4 %grid_first.1 = (bf16[1024,512]{1,0:T(8,128)(2,1)}, bf16[512,512]{1,0:T(8,128)(2,1)}) custom-call(bf16[1024,512]{1,0:T(8,128)(2,1)} %grid_ref.3, bf16[2,512,512]{2,1,0:T(8,128)(2,1)} %w1_ref.5, bf16[512,512]{1,0:T(8,128)(2,1)} %w2_ref.5), custom_call_target="tpu_custom_call" | custom-call | flops 536870912 | bytes 3145728 | tf_op jit(solution)/shard_map/grid_first/pallas_call | solution.py:465
  78.4 10.6 %all-to-all-done.2.received_ref = bf16[128,16,128]{2,1,0:T(8,128)(2,1)S(1)} async-done(((bf16[128,16,128]{2,1,0:T(8,128)(2,1)}), bf16[128,16,128]{2,1,0:T(8,128)(2,1)S(1)}, u32[]{:S(2)}, u32[]{:S(2)}) %all-to-all-start.2) | async-done | bytes 524320 | tf_op jit(solution)/shard_map/all_to_all | solution.py:463
  89.0 6.5 %decoder.1 = bf16[1024,512]{1,0:T(8,128)(2,1)} custom-call(s32[24,128]{1,0:T(8,128)S(1)} %reshape.48.ids_ref, bf16[1024,512]{1,0:T(8,128)(2,1)} %grid_ref.3, bf16[1024,512]{1,0:T(8,128)(2,1)} %get-tuple-element.20.half_ref, bf16[128,16,128]{2,1,0:T(8,128)(2,1)S(1)} %all-to-all-done.2.received_ref, bf16[512,512]{1,0:T(8,128)(2,1)} %get-tuple-element.22.w2_ref, ...), custom_call_target="tpu_custom_call" | custom-call | tf_op jit(solution)/shard_map/decoder/pallas_call | solution.py:483
  (23 shorter events, 0.1 us)
Async XLA Ops:
  0.6 12.8 %copy-start.11 = (s32[1,1,4096]{2,1,0:T(1,128)S(1)}, s32[1,1,4096]{2,1,0:T(1,128)}, u32[]{:S(2)}) copy-start(s32[1,1,4096]{2,1,0:T(1,128)} %param.21) | copy-start | bytes 49156
  0.6 12.8 %copy-start.10 = (s32[1,1,4096]{2,1,0:T(1,128)S(1)}, s32[1,1,4096]{2,1,0:T(1,128)}, u32[]{:S(2)}) copy-start(s32[1,1,4096]{2,1,0:T(1,128)} %param.22) | copy-start | bytes 49156
  3.2 24.1 %all-to-all-start = ((bf16[16,64,512]{2,1,0:T(8,128)(2,1)}), bf16[16,64,512]{2,1,0:T(8,128)(2,1)S(1)}, u32[]{:S(2)}, u32[]{:S(2)}) async-start(bf16[16,64,512]{2,1,0:T(8,128)(2,1)} %get-tuple-element.16), calls=%async_computation | async-start | bytes 2097152 | tf_op jit(solution)/shard_map/all_to_all | solution.py:367
  11.8 2.1 %collective-permute-start = (bf16[64,512]{1,0:T(8,128)(2,1)}, bf16[64,512]{1,0:T(8,128)(2,1)S(1)}, u32[]{:S(2)}, u32[]{:S(2)}) collective-permute-start(bf16[64,512]{1,0:T(8,128)(2,1)} %get-tuple-element.13), channel_id=1, source_target_pairs={{0,16},{16,0},{32,48},{48,32},{64,80},{80,64},{96,112},{112,96},{1... | collective-permute-start | bytes 196616 | tf_op jit(solution)/shard_map/ppermute | solution.py:369
  14.9 12.3 %collective-permute-start.1 = (bf16[128,512]{1,0:T(8,128)(2,1)S(1)}, bf16[128,512]{1,0:T(8,128)(2,1)S(1)}, u32[]{:S(2)}, u32[]{:S(2)}) collective-permute-start(bf16[128,512]{1,0:T(8,128)(2,1)S(1)} %maximum_select_fusion.near_ref), channel_id=1, source_target_pairs={{0,32},{16,48},{32,64},{48,80},{64,96},{80,112},{96,0},{112,16},{1... | collective-permute-start | bytes 393224 | tf_op jit(solution)/shard_map/ppermute | solution.py:377
  16.1 11.0 %collective-permute-start.2 = (bf16[128,512]{1,0:T(8,128)(2,1)S(1)}, bf16[128,512]{1,0:T(8,128)(2,1)S(1)}, u32[]{:S(2)}, u32[]{:S(2)}) collective-permute-start(bf16[128,512]{1,0:T(8,128)(2,1)S(1)} %maximum_select_fusion.near_ref), channel_id=1, source_target_pairs={{0,64},{16,80},{32,96},{48,112},{64,0},{80,16},{96,32},{112,48},{1... | collective-permute-start | bytes 393224 | tf_op jit(solution)/shard_map/ppermute | solution.py:377
  18.6 8.6 %collective-permute-start.3 = (bf16[128,512]{1,0:T(8,128)(2,1)S(1)}, bf16[128,512]{1,0:T(8,128)(2,1)S(1)}, u32[]{:S(2)}, u32[]{:S(2)}) collective-permute-start(bf16[128,512]{1,0:T(8,128)(2,1)S(1)} %maximum_select_fusion.near_ref), channel_id=1, source_target_pairs={{0,96},{16,112},{32,0},{48,16},{64,32},{80,48},{96,64},{112,80},{1... | collective-permute-start | bytes 393224 | tf_op jit(solution)/shard_map/ppermute | solution.py:377
  19.7 7.5 %copy-start.2 = (bf16[512,512]{1,0:T(8,128)(2,1)S(1)}, bf16[512,512]{1,0:T(8,128)(2,1)}, u32[]{:S(2)}) copy-start(bf16[512,512]{1,0:T(8,128)(2,1)} %w2_ref.3) | copy-start | bytes 1572868
  19.7 7.5 %copy-start.5 = (f32[512]{0:T(512)S(1)}, f32[512]{0:T(512)}, u32[]{:S(2)}) copy-start(f32[512]{0:T(512)} %param.28) | copy-start | bytes 6148
  27.3 39.7 %copy-start = (bf16[2,512,512]{2,1,0:T(8,128)(2,1)S(1)}, bf16[2,512,512]{2,1,0:T(8,128)(2,1)}, u32[]{:S(2)}) copy-start(bf16[2,512,512]{2,1,0:T(8,128)(2,1)} %w1_ref.5) | copy-start | bytes 3145732
  27.3 39.7 %copy-start.1 = (bf16[2,512,512]{2,1,0:T(8,128)(2,1)S(1)}, bf16[2,512,512]{2,1,0:T(8,128)(2,1)}, u32[]{:S(2)}) copy-start(bf16[2,512,512]{2,1,0:T(8,128)(2,1)} %w1_ref.4) | copy-start | bytes 3145732
  27.3 39.7 %copy-start.3 = (bf16[512,512]{1,0:T(8,128)(2,1)S(1)}, bf16[512,512]{1,0:T(8,128)(2,1)}, u32[]{:S(2)}) copy-start(bf16[512,512]{1,0:T(8,128)(2,1)} %w2_ref.4) | copy-start | bytes 1572868
  27.3 39.7 %copy-start.4 = (bf16[64,512]{1,0:T(8,128)(2,1)S(1)}, bf16[64,512]{1,0:T(8,128)(2,1)}, u32[]{:S(2)}) copy-start(bf16[64,512]{1,0:T(8,128)(2,1)} %nodes_ref.3) | copy-start | bytes 196612
  27.3 39.7 %copy-start.6 = (f32[512]{0:T(512)S(1)}, f32[512]{0:T(512)}, u32[]{:S(2)}) copy-start(f32[512]{0:T(512)} %param.31) | copy-start | bytes 6148
  27.3 39.7 %copy-start.7 = (s32[1,128,4]{1,2,0:T(4,128)S(1)}, s32[1,128,4]{1,2,0:T(4,128)}, u32[]{:S(2)}) copy-start(s32[1,128,4]{1,2,0:T(4,128)} %param.33) | copy-start | bytes 6148
  41.7 33.2 %copy-start.9 = (s32[1024,3]{0,1:T(4,128)S(1)}, s32[1024,3]{0,1:T(4,128)}, u32[]{:S(2)}) copy-start(s32[1024,3]{0,1:T(4,128)} %param.34) | copy-start | bytes 36868
  67.0 22.0 %copy-start.8 = (f32[512]{0:T(512)S(1)}, f32[512]{0:T(512)}, u32[]{:S(2)}) copy-start(f32[512]{0:T(512)} %param.37) | copy-start | bytes 6148
  69.2 19.8 %all-to-all-start.2 = ((bf16[128,16,128]{2,1,0:T(8,128)(2,1)}), bf16[128,16,128]{2,1,0:T(8,128)(2,1)S(1)}, u32[]{:S(2)}, u32[]{:S(2)}) async-start(bf16[128,16,128]{2,1,0:T(8,128)(2,1)} %get-tuple-element.21), calls=%async_computation.2 | async-start | bytes 1048576 | tf_op jit(solution)/shard_map/all_to_all | solution.py:463

commit v6 on v5

--- a/solution.py
+++ b/solution.py
@@ -80,16 +80,20 @@
     ]
     for copy in copies[:AHEAD]:
         copy.start()
+    levels, width = bias_ref.shape
+    bias = bias_ref[...].astype(jnp.float32)
+    bias = jnp.concatenate([bias, jnp.zeros((LANES - levels, width), jnp.float32)], axis=0)
     weight_copy.wait()
+    joined = jnp.concatenate([weight[...], bias.astype(jnp.bfloat16)], axis=0)
     outs = []
     for k in range(blocks):
         columns = jnp.transpose(ids_ref[k])
-        hot = stacked_hot(columns, 0, ids_ref.shape[1], bias_ref.shape[0])
+        hot = stacked_hot(columns, 0, ids_ref.shape[1], LANES)
         copies[k].wait()
         if k + AHEAD < blocks:
             copies[k + AHEAD].start()
         part = slice(k * span, (k + 1) * span)
-        product = dot(rows[part, :], weight[...]) + dot(hot, bias_ref[...])
+        product = dot(jnp.concatenate([rows[part, :], hot], axis=1), joined)
         half[part, :] = (0.5 * product).astype(jnp.bfloat16)
         place = pl.ds(k * span, span)
         outs.append(pltpu.make_async_copy(half.at[place], half_ref.at[place], half_sems.at[k]))
@@ -209,7 +213,18 @@
 
 
 def node_kernel(
-    parts_ref, nodes_ref, w1_ref, w2_ref, gain_ref, dec_w1_ref, picks_ref, out_ref, picked_ref, wide
+    parts_ref,
+    nodes_ref,
+    w1_ref,
+    w2_ref,
+    gain_ref,
+    dec_w1_ref,
+    picks_ref,
+    out_ref,
+    picked_ref,
+    wide,
+    picked,
+    sems,
 ):
     low = jnp.sum(parts_ref[...].astype(jnp.float32), axis=0).astype(jnp.bfloat16)
     nodes = nodes_ref[...]
@@ -221,13 +236,23 @@
     peers, strips, _ = picked_ref.shape
     columns = jnp.transpose(picks_ref[...])
     groups = strips // picks_ref.shape[0]
-    for j in range(picks_ref.shape[0]):
-        chosen = dot(column_hot(columns[:, j : j + 1], nodes.shape[0]), projected)
-        for q in range(groups):
-            wide[pl.ds(j * groups + q, peers, stride=strips), :] = chosen[
-                :, q * LANES : (q + 1) * LANES
-            ]
-    picked_ref[...] = wide[...].reshape(picked_ref.shape).astype(jnp.bfloat16)
+    span = peers // sems.shape[0]
+    copies = []
+    for h in range(sems.shape[0]):
+        for j in range(picks_ref.shape[0]):
+            ids = columns[h * span : (h + 1) * span, j : j + 1]
+            chosen = dot(column_hot(ids, nodes.shape[0]), projected)
+            for q in range(groups):
+                wide[pl.ds(h * span * strips + j * groups + q, span, stride=strips), :] = chosen[
+                    :, q * LANES : (q + 1) * LANES
+                ]
+        half = wide[h * span * strips : (h + 1) * span * strips, :]
+        place = pl.ds(h * span, span)
+        picked[place] = half.reshape(span, strips, LANES).astype(jnp.bfloat16)
+        copies.append(pltpu.make_async_copy(picked.at[place], picked_ref.at[place], sems.at[h]))
+        copies[-1].start()
+    for copy in copies:
+        copy.wait()
 
 
 def decode_kernel(
@@ -449,13 +474,17 @@
         ],
         out_specs=(
             pl.BlockSpec((block, width), lambda i: (0, 0)),
-            pl.BlockSpec((peers, strips, LANES), lambda i: (0, 0, 0)),
+            hbm,
         ),
         out_shape=(
             jax.ShapeDtypeStruct((block, width), bf16),
             jax.ShapeDtypeStruct((peers, strips, LANES), bf16),
         ),
-        scratch_shapes=[pltpu.VMEM((peers * strips, LANES), f32)],
+        scratch_shapes=[
+            pltpu.VMEM((peers * strips, LANES), f32),
+            pltpu.VMEM((peers, strips, LANES), bf16),
+            pltpu.SemaphoreType.DMA((2,)),
+        ],
         compiler_params=params(12),
         name="nodes",
     )(node_parts, nodes, node_w1, node_w2, node_scale, dec_w1, picks)

time: 95.2 us -> 96.9 us (1.018)
  blocking collectives: 25.2 us -> 28.6 us
  Pallas kernels: 36.4 us -> 33.8 us
    all_to_all x1, blocking collectives: 25.2 us -> 28.6 us  [on_device(): lax.all_to_all(partial_sum.reshape(col_size, block, width), 'col', 0, 0,...]
    pallas_call x1, Pallas kernels: 14.4 us -> 11.1 us  [on_device(): pl.pallas_call(edge_kernel, in_specs=[smem, vmem, hbm, hbm] + [vmem] * (4...]
  transfers between devices with their start and end apart: 6 -> 6, of which waited for: 3 -> 2; matrix products, arithmetic and copies ran while one was open for 1% -> 1% of each run, Pallas kernels for 11% -> 11%
where the time goes in v6:
time: 96.9 us; the launch traced here: 96.4 us
  Pallas kernels  33.8 us (35%)
  blocking collectives  28.6 us (30%)
  starting transfers between devices  20.3 us (21%)
  waiting for transfers between devices  10.9 us (11%)
  between operations  1.68 us (2%)
  other arithmetic  1.03 us (1%)
    all_to_all x1, blocking collectives, on_device(): lax.all_to_all(partial_sum.reshape(col_size, block, width), 'col', 0, 0,...  28.6 us
    pallas_call x1, Pallas kernels, on_device(): pl.pallas_call(edge_kernel, in_specs=[smem, vmem, hbm, hbm] + [vmem] * (4...  11.1 us
    all_to_all x1, waiting for transfers between devices, on_device(): received = lax.all_to_all(picked, ('row', 'col'), 0, 0, tiled=True)  10.6 us
    all_to_all x1, starting transfers between devices, on_device(): lax.all_to_all(recv_copies, 'col', 0, 0, tiled=True).reshape(-1, width)  8.6 us
    pallas_call x1, Pallas kernels, on_device(): pl.pallas_call(edge_first_kernel, in_specs=[vmem, hbm, hbm, vmem], out_sp...  7.6 us
    pallas_call x1, Pallas kernels, on_device(): pl.pallas_call(decode_kernel, in_specs=[vmem] + [hbm] * 4 + [vmem], out_s...  6.5 us
    all_to_all x1, starting transfers between devices, on_device(): received = lax.all_to_all(picked, ('row', 'col'), 0, 0, tiled=True)  5.81 us
    ppermute x3, starting transfers between devices, on_device(): lax.ppermute(near, 'row', [(i, (i + 2 * k) % row_size) for i in range(row...  4.88 us
  transfers between devices with their start and end apart: 6, of which 2 were waited for; matrix products, arithmetic and copies ran while one was open for 1% of the time, Pallas kernels for 11%

profile of v6, /device:TPU:1, one launch (start us, length us, event | category | flops | bytes accessed | tf_op | source)
XLA Modules:
  0.0 96.4 jit_solution(5082843660791790792)
XLA Ops:
  0.7 2.5 %project.1 = (bf16[64,512]{1,0:T(8,128)(2,1)}, bf16[16,64,512]{2,1,0:T(8,128)(2,1)}) custom-call(bf16[64,512]{1,0:T(8,128)(2,1)} %nodes_ref.3, bf16[3,512,512]{2,1,0:T(8,128)(2,1)} %w1_ref.3, bf16[3,512,512]{2,1,0:T(8,128)(2,1)} %w1_ref.3), custom_call_target="tpu_custom_call" | custom-call | tf_op jit(solution)/shard_map/project/pallas_call | solution.py:377
  3.2 8.6 %all-to-all-start = ((bf16[16,64,512]{2,1,0:T(8,128)(2,1)}), bf16[16,64,512]{2,1,0:T(8,128)(2,1)S(1)}, u32[]{:S(2)}, u32[]{:S(2)}) async-start(bf16[16,64,512]{2,1,0:T(8,128)(2,1)} %get-tuple-element.16), calls=%async_computation | async-start | bytes 2097152 | tf_op jit(solution)/shard_map/all_to_all | solution.py:392
  11.8 1.0 %collective-permute-start = (bf16[64,512]{1,0:T(8,128)(2,1)}, bf16[64,512]{1,0:T(8,128)(2,1)S(1)}, u32[]{:S(2)}, u32[]{:S(2)}) collective-permute-start(bf16[64,512]{1,0:T(8,128)(2,1)} %get-tuple-element.13), channel_id=1, source_target_pairs={{0,16},{16,0},{32,48},{48,32},{64,80},{80,64},{96,112},{112,96},{1... | collective-permute-start | bytes 196616 | tf_op jit(solution)/shard_map/ppermute | solution.py:394
  13.5 0.1 pad_add_fusion.1.place_ref
  13.6 0.3 collective-permute-done
  13.9 0.9 maximum_select_fusion.near_ref
  14.9 1.3 %collective-permute-start.1 = (bf16[128,512]{1,0:T(8,128)(2,1)S(1)}, bf16[128,512]{1,0:T(8,128)(2,1)S(1)}, u32[]{:S(2)}, u32[]{:S(2)}) collective-permute-start(bf16[128,512]{1,0:T(8,128)(2,1)S(1)} %maximum_select_fusion.near_ref), channel_id=1, source_target_pairs={{0,32},{16,48},{32,64},{48,80},{64,96},{80,112},{96,0},{112,16},{1... | collective-permute-start | bytes 393224 | tf_op jit(solution)/shard_map/ppermute | solution.py:402
  16.1 2.4 %collective-permute-start.2 = (bf16[128,512]{1,0:T(8,128)(2,1)S(1)}, bf16[128,512]{1,0:T(8,128)(2,1)S(1)}, u32[]{:S(2)}, u32[]{:S(2)}) collective-permute-start(bf16[128,512]{1,0:T(8,128)(2,1)S(1)} %maximum_select_fusion.near_ref), channel_id=1, source_target_pairs={{0,64},{16,80},{32,96},{48,112},{64,0},{80,16},{96,32},{112,48},{1... | collective-permute-start | bytes 393224 | tf_op jit(solution)/shard_map/ppermute | solution.py:402
  18.6 1.2 %collective-permute-start.3 = (bf16[128,512]{1,0:T(8,128)(2,1)S(1)}, bf16[128,512]{1,0:T(8,128)(2,1)S(1)}, u32[]{:S(2)}, u32[]{:S(2)}) collective-permute-start(bf16[128,512]{1,0:T(8,128)(2,1)S(1)} %maximum_select_fusion.near_ref), channel_id=1, source_target_pairs={{0,96},{16,112},{32,0},{48,16},{64,32},{80,48},{96,64},{112,80},{1... | collective-permute-start | bytes 393224 | tf_op jit(solution)/shard_map/ppermute | solution.py:402
  19.7 7.6 %edge_first.1.half_ref = bf16[4096,512]{1,0:T(8,128)(2,1)} custom-call(s32[4,8,128]{2,1,0:T(8,128)} %bitcast.25, bf16[4096,512]{1,0:T(8,128)(2,1)} %bitcast.23, bf16[3,512,512]{2,1,0:T(8,128)(2,1)} %w1_ref.3, bf16[7,512]{1,0:T(8,128)(2,1)} %bias_ref.1), custom_call_target="tpu_custom_call" | custom-call | flops 2147483648 | bytes 4194304 | tf_op jit(solution)/shard_map/edge_first/pallas_call | solution.py:409
  27.4 0.0 copy-start
  27.4 0.0 copy-start.1
  27.4 0.0 copy-start.3
  27.5 0.0 copy-start.4
  27.5 0.0 copy-start.6
  27.5 0.0 copy-start.7
  27.5 11.1 %edges.1 = (bf16[4096,512]{1,0:T(8,128)(2,1)}, bf16[1024,512]{1,0:T(8,128)(2,1)S(1)}) custom-call(s32[2]{0:T(128)S(1)} %pad_add_fusion.1.place_ref, s32[4,16,128]{2,1,0:T(8,128)S(1)} %pad_add_fusion.ids_ref, bf16[4096,512]{1,0:T(8,128)(2,1)} %bitcast.24, bf16[4096,512]{1,0:T(8,128)(2,1)} %edge_first.1.half_ref, ...), custom_call_target="tpu_custom_call" | custom-call | tf_op jit(solution)/shard_map/edges/pallas_call | solution.py:435
  38.6 0.0 copy-start.9
  38.6 28.6 %all_to_all.15.parts_ref = bf16[16,64,512]{2,1,0:T(8,128)(2,1)S(1)} all-to-all(bf16[16,64,512]{2,1,0:T(8,128)(2,1)S(1)} %bitcast.18), channel_id=1, replica_groups=mesh['row'=8,'col'=16] {'col'}, dimensions={0} | all-to-all | bytes 2097152 | tf_op jit(solution)/shard_map/all_to_all | solution.py:457
  67.2 2.7 %nodes.1 = (bf16[64,512]{1,0:T(8,128)(2,1)}, bf16[128,16,128]{2,1,0:T(8,128)(2,1)}) custom-call(bf16[16,64,512]{2,1,0:T(8,128)(2,1)S(1)} %all_to_all.15.parts_ref, bf16[64,512]{1,0:T(8,128)(2,1)S(1)} %copy-done.4, bf16[2,512,512]{2,1,0:T(8,128)(2,1)S(1)} %copy-done.1, bf16[512,512]{1,0:T(8,128)(2,1)S(1)} %copy-done.3, f32[1,512]{1,0:T(1,128)S(1)} %bitcast.20, ...), custom_call_target="tpu_custom_call" | custom-call | tf_op jit(solution)/shard_map/nodes/pallas_call | solution.py:463
  69.9 5.8 %all-to-all-start.2 = ((bf16[128,16,128]{2,1,0:T(8,128)(2,1)}), bf16[128,16,128]{2,1,0:T(8,128)(2,1)S(1)}, u32[]{:S(2)}, u32[]{:S(2)}) async-start(bf16[128,16,128]{2,1,0:T(8,128)(2,1)} %get-tuple-element.21), calls=%async_computation.2 | async-start | bytes 1048576 | tf_op jit(solution)/shard_map/all_to_all | solution.py:492
  75.8 3.4 %grid_first.1 = (bf16[1024,512]{1,0:T(8,128)(2,1)}, bf16[512,512]{1,0:T(8,128)(2,1)}) custom-call(bf16[1024,512]{1,0:T(8,128)(2,1)} %grid_ref.3, bf16[2,512,512]{2,1,0:T(8,128)(2,1)} %w1_ref.5, bf16[512,512]{1,0:T(8,128)(2,1)} %w2_ref.5), custom_call_target="tpu_custom_call" | custom-call | flops 536870912 | bytes 3145728 | tf_op jit(solution)/shard_map/grid_first/pallas_call | solution.py:494
  79.2 10.6 %all-to-all-done.2.received_ref = bf16[128,16,128]{2,1,0:T(8,128)(2,1)S(1)} async-done(((bf16[128,16,128]{2,1,0:T(8,128)(2,1)}), bf16[128,16,128]{2,1,0:T(8,128)(2,1)S(1)}, u32[]{:S(2)}, u32[]{:S(2)}) %all-to-all-start.2) | async-done | bytes 524320 | tf_op jit(solution)/shard_map/all_to_all | solution.py:492
  89.7 6.5 %decoder.1 = bf16[1024,512]{1,0:T(8,128)(2,1)} custom-call(s32[24,128]{1,0:T(8,128)S(1)} %reshape.48.ids_ref, bf16[1024,512]{1,0:T(8,128)(2,1)} %grid_ref.3, bf16[1024,512]{1,0:T(8,128)(2,1)} %get-tuple-element.20.half_ref, bf16[128,16,128]{2,1,0:T(8,128)(2,1)S(1)} %all-to-all-done.2.received_ref, bf16[512,512]{1,0:T(8,128)(2,1)} %get-tuple-element.22.w2_ref, ...), custom_call_target="tpu_custom_call" | custom-call | tf_op jit(solution)/shard_map/decoder/pallas_call | solution.py:512
  (23 shorter events, 0.1 us)
Async XLA Ops:
  0.6 12.8 %copy-start.11 = (s32[1,1,4096]{2,1,0:T(1,128)S(1)}, s32[1,1,4096]{2,1,0:T(1,128)}, u32[]{:S(2)}) copy-start(s32[1,1,4096]{2,1,0:T(1,128)} %param.21) | copy-start | bytes 49156
  0.6 12.8 %copy-start.10 = (s32[1,1,4096]{2,1,0:T(1,128)S(1)}, s32[1,1,4096]{2,1,0:T(1,128)}, u32[]{:S(2)}) copy-start(s32[1,1,4096]{2,1,0:T(1,128)} %param.22) | copy-start | bytes 49156
  3.2 24.2 %all-to-all-start = ((bf16[16,64,512]{2,1,0:T(8,128)(2,1)}), bf16[16,64,512]{2,1,0:T(8,128)(2,1)S(1)}, u32[]{:S(2)}, u32[]{:S(2)}) async-start(bf16[16,64,512]{2,1,0:T(8,128)(2,1)} %get-tuple-element.16), calls=%async_computation | async-start | bytes 2097152 | tf_op jit(solution)/shard_map/all_to_all | solution.py:392
  11.8 2.1 %collective-permute-start = (bf16[64,512]{1,0:T(8,128)(2,1)}, bf16[64,512]{1,0:T(8,128)(2,1)S(1)}, u32[]{:S(2)}, u32[]{:S(2)}) collective-permute-start(bf16[64,512]{1,0:T(8,128)(2,1)} %get-tuple-element.13), channel_id=1, source_target_pairs={{0,16},{16,0},{32,48},{48,32},{64,80},{80,64},{96,112},{112,96},{1... | collective-permute-start | bytes 196616 | tf_op jit(solution)/shard_map/ppermute | solution.py:394
  14.9 12.5 %collective-permute-start.1 = (bf16[128,512]{1,0:T(8,128)(2,1)S(1)}, bf16[128,512]{1,0:T(8,128)(2,1)S(1)}, u32[]{:S(2)}, u32[]{:S(2)}) collective-permute-start(bf16[128,512]{1,0:T(8,128)(2,1)S(1)} %maximum_select_fusion.near_ref), channel_id=1, source_target_pairs={{0,32},{16,48},{32,64},{48,80},{64,96},{80,112},{96,0},{112,16},{1... | collective-permute-start | bytes 393224 | tf_op jit(solution)/shard_map/ppermute | solution.py:402
  16.1 11.2 %collective-permute-start.2 = (bf16[128,512]{1,0:T(8,128)(2,1)S(1)}, bf16[128,512]{1,0:T(8,128)(2,1)S(1)}, u32[]{:S(2)}, u32[]{:S(2)}) collective-permute-start(bf16[128,512]{1,0:T(8,128)(2,1)S(1)} %maximum_select_fusion.near_ref), channel_id=1, source_target_pairs={{0,64},{16,80},{32,96},{48,112},{64,0},{80,16},{96,32},{112,48},{1... | collective-permute-start | bytes 393224 | tf_op jit(solution)/shard_map/ppermute | solution.py:402
  18.6 8.8 %collective-permute-start.3 = (bf16[128,512]{1,0:T(8,128)(2,1)S(1)}, bf16[128,512]{1,0:T(8,128)(2,1)S(1)}, u32[]{:S(2)}, u32[]{:S(2)}) collective-permute-start(bf16[128,512]{1,0:T(8,128)(2,1)S(1)} %maximum_select_fusion.near_ref), channel_id=1, source_target_pairs={{0,96},{16,112},{32,0},{48,16},{64,32},{80,48},{96,64},{112,80},{1... | collective-permute-start | bytes 393224 | tf_op jit(solution)/shard_map/ppermute | solution.py:402
  19.7 7.7 %copy-start.2 = (bf16[512,512]{1,0:T(8,128)(2,1)S(1)}, bf16[512,512]{1,0:T(8,128)(2,1)}, u32[]{:S(2)}) copy-start(bf16[512,512]{1,0:T(8,128)(2,1)} %w2_ref.3) | copy-start | bytes 1572868
  19.7 7.7 %copy-start.5 = (f32[512]{0:T(512)S(1)}, f32[512]{0:T(512)}, u32[]{:S(2)}) copy-start(f32[512]{0:T(512)} %param.28) | copy-start | bytes 6148
  27.4 39.7 %copy-start = (bf16[2,512,512]{2,1,0:T(8,128)(2,1)S(1)}, bf16[2,512,512]{2,1,0:T(8,128)(2,1)}, u32[]{:S(2)}) copy-start(bf16[2,512,512]{2,1,0:T(8,128)(2,1)} %w1_ref.5) | copy-start | bytes 3145732
  27.4 39.7 %copy-start.1 = (bf16[2,512,512]{2,1,0:T(8,128)(2,1)S(1)}, bf16[2,512,512]{2,1,0:T(8,128)(2,1)}, u32[]{:S(2)}) copy-start(bf16[2,512,512]{2,1,0:T(8,128)(2,1)} %w1_ref.4) | copy-start | bytes 3145732
  27.4 39.7 %copy-start.3 = (bf16[512,512]{1,0:T(8,128)(2,1)S(1)}, bf16[512,512]{1,0:T(8,128)(2,1)}, u32[]{:S(2)}) copy-start(bf16[512,512]{1,0:T(8,128)(2,1)} %w2_ref.4) | copy-start | bytes 1572868
  27.5 39.7 %copy-start.4 = (bf16[64,512]{1,0:T(8,128)(2,1)S(1)}, bf16[64,512]{1,0:T(8,128)(2,1)}, u32[]{:S(2)}) copy-start(bf16[64,512]{1,0:T(8,128)(2,1)} %nodes_ref.3) | copy-start | bytes 196612
  27.5 39.7 %copy-start.6 = (f32[512]{0:T(512)S(1)}, f32[512]{0:T(512)}, u32[]{:S(2)}) copy-start(f32[512]{0:T(512)} %param.31) | copy-start | bytes 6148
  27.5 39.7 %copy-start.7 = (s32[1,128,4]{1,2,0:T(4,128)S(1)}, s32[1,128,4]{1,2,0:T(4,128)}, u32[]{:S(2)}) copy-start(s32[1,128,4]{1,2,0:T(4,128)} %param.33) | copy-start | bytes 6148
  38.6 37.2 %copy-start.9 = (s32[1024,3]{0,1:T(4,128)S(1)}, s32[1024,3]{0,1:T(4,128)}, u32[]{:S(2)}) copy-start(s32[1024,3]{0,1:T(4,128)} %param.34) | copy-start | bytes 36868
  67.1 22.6 %copy-start.8 = (f32[512]{0:T(512)S(1)}, f32[512]{0:T(512)}, u32[]{:S(2)}) copy-start(f32[512]{0:T(512)} %param.37) | copy-start | bytes 6148
  69.9 19.8 %all-to-all-start.2 = ((bf16[128,16,128]{2,1,0:T(8,128)(2,1)}), bf16[128,16,128]{2,1,0:T(8,128)(2,1)S(1)}, u32[]{:S(2)}, u32[]{:S(2)}) async-start(bf16[128,16,128]{2,1,0:T(8,128)(2,1)} %get-tuple-element.21), calls=%async_computation.2 | async-start | bytes 1048576 | tf_op jit(solution)/shard_map/all_to_all | solution.py:492
